TPU v7x, 32 devices: a whole 2x2x4 slice. The times are simulated.
32 devices in a mesh: ctx: 8 (over z, core), head: 4 (over y, x).
Axes of the slice: x: 2, y: 2, z: 4, core: 2. Of those that a mesh axis runs over, the one named last changes fastest.
Arguments:
- queries: bfloat16 [2048, 32, 128], P('ctx', 'head'), may hold values from -8 to 8
- key_proj: bfloat16 [2048, 4, 128], P(('ctx', 'head')), may hold values from -8 to 8
- value_proj: bfloat16 [2048, 4, 128], P(('ctx', 'head')), may hold values from -6 to 6
- out_grad: bfloat16 [2048, 32, 128], P('ctx', 'head'), may hold values from -6 to 6
- tile_order: int32 [16], replicated, may hold values from 0 to 15, each once
- doc_tiles: int32 [4], replicated, may hold values from 1 to 8, 16 in all
Outputs:
- attended: bfloat16 [2048, 32, 128], P('ctx', 'head')
- query_grad: bfloat16 [2048, 32, 128], P('ctx', 'head')
- key_grad: bfloat16 [2048, 4, 128], P(('ctx', 'head'))
- value_grad: bfloat16 [2048, 4, 128], P(('ctx', 'head'))
Inputs may be any that keep to these rules, and one draw needn't show every extreme that they name: `tile_order`: a permutation of the 16 tiles. `doc_tiles`: positive lengths in tiles summing to 16.
All inputs are finite; a program needn't handle non-finite values.
Results may differ from a plain program's by a relative error of at most 0.02.
Values may be sent and summed in bfloat16 or wider, within the bound.
A program may use at most 64 MiB of HBM per device.

v0:
```python
import math

import jax
import jax.numpy as jnp
from jax import lax
from jax.sharding import PartitionSpec as P

TILE = 128


NEG = -1e30


def from_behind(value, axis, steps):
    count = lax.axis_size(axis)
    pairs = [(source, (source + steps) % count) for source in range(count)]
    return lax.ppermute(value, axis, pairs)


def row_info(tile_order, doc_ends, shard, row_count, tile_len):
    per_shard = row_count // tile_len
    shard_tiles = lax.dynamic_slice_in_dim(tile_order, shard * per_shard, per_shard)
    tile_doc = jnp.sum((shard_tiles[:, None] >= doc_ends[None, :]).astype(jnp.int32), axis=1)
    offsets = jnp.arange(tile_len, dtype=jnp.int32)
    positions = (shard_tiles[:, None] * tile_len + offsets[None, :]).reshape(-1)
    documents = jnp.broadcast_to(tile_doc[:, None], (per_shard, tile_len)).reshape(-1)
    return (positions, documents, shard_tiles, tile_doc)


def block_scores(query_block, key_block, score_scale):
    return (
        jnp.einsum("tngd,knd->tngk", query_block, key_block, preferred_element_type=jnp.float32)
        * score_scale
    )


def forward_block(carried, query_block, key_block, value_block, allowed, score_scale):
    running_max, running_sum, accumulated = carried
    scores = block_scores(query_block, key_block, score_scale)
    visible = allowed[:, None, None, :]
    block_max = jnp.max(jnp.where(visible, scores, NEG), axis=-1)
    new_max = jnp.maximum(running_max, block_max)
    weights = jnp.where(visible, jnp.exp(scores - new_max[..., None]), 0.0)
    factor = jnp.exp(running_max - new_max)
    running_sum = running_sum * factor + jnp.sum(weights, axis=-1)
    product = jnp.einsum(
        "tngk,knd->tngd",
        weights.astype(jnp.bfloat16),
        value_block,
        preferred_element_type=jnp.float32,
    )
    accumulated = accumulated * factor[..., None] + product
    return (new_max, running_sum, accumulated)


def backward_block(
    query_block, grad_block, log_sum, delta, key_block, value_block, allowed, score_scale
):
    scores = block_scores(query_block, key_block, score_scale)
    visible = allowed[:, None, None, :]
    probs = jnp.where(visible, jnp.exp(scores - log_sum[..., None]), 0.0)
    value_add = jnp.einsum(
        "tngk,tngd->knd", probs.astype(jnp.bfloat16), grad_block, preferred_element_type=jnp.float32
    )
    dprobs = jnp.einsum(
        "tngd,knd->tngk", grad_block, value_block, preferred_element_type=jnp.float32
    )
    dscores = (probs * (dprobs - delta[..., None])).astype(jnp.bfloat16)
    query_add = jnp.einsum("tngk,knd->tngd", dscores, key_block, preferred_element_type=jnp.float32)
    key_add = jnp.einsum("tngk,tngd->knd", dscores, query_block, preferred_element_type=jnp.float32)
    return (query_add, key_add, value_add)


def body(queries, key_proj, value_proj, out_grad, tile_order, doc_tiles):
    key_rows, value_rows = (
        lax.all_to_all(key_proj, "head", split_axis=1, concat_axis=0, tiled=True),
        lax.all_to_all(value_proj, "head", split_axis=1, concat_axis=0, tiled=True),
    )
    row_count = queries.shape[0]
    kv_local = key_rows.shape[1]
    group_size = queries.shape[1] // kv_local
    depth = queries.shape[2]
    query_rows = queries.reshape(row_count, kv_local, group_size, depth)
    grad_rows = out_grad.reshape(row_count, kv_local, group_size, depth)
    score_scale = 1.0 / math.sqrt(depth)
    cycle_size = lax.axis_size("ctx")
    my_shard = lax.axis_index("ctx")
    doc_ends = jnp.cumsum(doc_tiles)
    query_pos, query_doc, query_tiles, query_tdoc = row_info(
        tile_order, doc_ends, my_shard, row_count, TILE
    )

    def block_mask(shard):
        key_pos, key_doc, key_tiles, key_tdoc = row_info(
            tile_order, doc_ends, shard, row_count, TILE
        )
        allowed = (query_doc[:, None] == key_doc[None, :]) & (
            key_pos[None, :] <= query_pos[:, None]
        )
        reached = jnp.any(
            (query_tdoc[:, None] == key_tdoc[None, :])
            & (key_tiles[None, :] <= query_tiles[:, None])
        )
        return (allowed, reached)

    def forward_step(carried, key_block, value_block, shard):
        allowed, reached = block_mask(shard)
        return forward_block(carried, query_rows, key_block, value_block, allowed, score_scale)

    stats_shape = (row_count, kv_local, group_size)
    initial = (
        jnp.full(stats_shape, NEG, jnp.float32),
        jnp.zeros(stats_shape, jnp.float32),
        jnp.zeros(stats_shape + (depth,), jnp.float32),
    )
    first = forward_step(initial, key_rows, value_rows, my_shard)

    def forward_turn(turn_index, carried):
        key_block, value_block = from_behind((carried[0], carried[1]), "ctx", 1)
        shard = (my_shard - turn_index) % cycle_size
        return (key_block, value_block, forward_step(carried[2], key_block, value_block, shard))

    finished = lax.fori_loop(1, cycle_size, forward_turn, (key_rows, value_rows, first))
    running_max, running_sum, accumulated = finished[2]
    attended = (accumulated / running_sum[..., None]).astype(jnp.bfloat16)
    log_sum = running_max + jnp.log(running_sum)
    delta = jnp.sum(grad_rows.astype(jnp.float32) * attended.astype(jnp.float32), axis=-1)

    def backward_step(key_block, value_block, shard):
        allowed, reached = block_mask(shard)
        return backward_block(
            query_rows, grad_rows, log_sum, delta, key_block, value_block, allowed, score_scale
        )

    query_acc = jnp.zeros(stats_shape + (depth,), jnp.float32)

    def backward_turn(turn_index, carried):
        key_block, value_block, key_acc, value_acc, query_sum = carried
        shard = (my_shard - turn_index) % cycle_size
        query_add, key_add, value_add = backward_step(key_block, value_block, shard)
        key_block, value_block = from_behind((key_block, value_block), "ctx", 1)
        key_acc, value_acc = (
            from_behind((key_acc + key_add).astype(jnp.bfloat16), "ctx", 1).astype(jnp.float32),
            from_behind((value_acc + value_add).astype(jnp.bfloat16), "ctx", 1).astype(jnp.float32),
        )
        return (key_block, value_block, key_acc, value_acc, query_sum + query_add)

    grad_zero = jnp.zeros((row_count, kv_local, depth), jnp.float32)
    finished = lax.fori_loop(
        0, cycle_size, backward_turn, (key_rows, value_rows, grad_zero, grad_zero, query_acc)
    )
    key_acc, value_acc, query_acc = (finished[2], finished[3], finished[4])
    query_grad = (
        (query_acc * score_scale)
        .astype(jnp.bfloat16)
        .reshape(row_count, kv_local * group_size, depth)
    )
    key_grad = (key_acc * score_scale).astype(jnp.bfloat16)
    value_grad = value_acc.astype(jnp.bfloat16)
    attended = attended.reshape(row_count, kv_local * group_size, depth)
    key_back, value_back = (
        lax.all_to_all(key_grad, "head", split_axis=0, concat_axis=1, tiled=True),
        lax.all_to_all(value_grad, "head", split_axis=0, concat_axis=1, tiled=True),
    )
    return (attended, query_grad, key_back, value_back)


def solution(mesh):
    in_specs = (
        P("ctx", "head", None),
        P(("ctx", "head"), None, None),
        P(("ctx", "head"), None, None),
        P("ctx", "head", None),
        P(),
        P(),
    )
    out_specs = (
        P("ctx", "head", None),
        P("ctx", "head", None),
        P(("ctx", "head"), None, None),
        P(("ctx", "head"), None, None),
    )
    return jax.shard_map(body, mesh=mesh, in_specs=in_specs, out_specs=out_specs, check_vma=False)
```

profile of v0, /device:TPU:0, one launch (start us, length us, event | category | flops | bytes accessed | tf_op | source)
XLA Modules:
  0.0 183.4 jit_solution(8842191101418843890)
XLA Ops:
  0.6 1.5 copy.74
  2.2 5.2 %all-to-all-start = ((bf16[64,4,128]{2,0,1:T(8,128)(2,1)}), bf16[64,4,128]{2,0,1:T(8,128)(2,1)S(1)}, u32[]{:S(2)}, u32[]{:S(2)}) async-start(bf16[64,4,128]{2,0,1:T(8,128)(2,1)} %copy.74), calls=%async_computation | async-start | bytes 131072 | tf_op jit(solution)/shard_map/all_to_all | solution.py:76
  9.6 1.5 copy.75
  12.2 3.3 %all-to-all-start.1 = ((bf16[64,4,128]{2,0,1:T(8,128)(2,1)}), bf16[64,4,128]{2,0,1:T(8,128)(2,1)S(1)}, u32[]{:S(2)}, u32[]{:S(2)}) async-start(bf16[64,4,128]{2,0,1:T(8,128)(2,1)} %copy.75), calls=%async_computation.1 | async-start | bytes 131072 | tf_op jit(solution)/shard_map/all_to_all | solution.py:77
  18.5 1.8 all-to-all-done.1
  22.9 62.3 %while.48 = (s32[]{:T(128)}, bf16[256,1,128]{2,0,1:T(8,128)(2,1)}, bf16[256,1,128]{2,0,1:T(8,128)(2,1)}, f32[256,1,8]{0,2,1:T(8,128)S(1)}, f32[256,1,8]{0,2,1:T(...) while((s32[]{:T(128)}, bf16[256,1,128]{2,0,1:T(8,128)(2,1)}, ...), condition=%wide.region_8.9_spmd.clone, body=%wide.region_4.0_spmd.clone.sunk | while | flops 274930240 | bytes 10232312 | solution.py:123
  22.9 1.7 collective-permute-start.1
  24.6 1.3 add_bitcast_fusion.9
  31.8 1.5 collective-permute-start.1
  33.3 1.3 add_bitcast_fusion.9
  40.7 1.3 collective-permute-start.1
  42.0 1.3 add_bitcast_fusion.9
  49.7 1.3 add_bitcast_fusion.9
  53.5 1.8 collective-permute-done
  58.6 1.3 add_bitcast_fusion.9
  62.4 1.8 collective-permute-done
  67.5 1.3 add_bitcast_fusion.9
  71.3 1.8 collective-permute-done
  76.4 1.3 add_bitcast_fusion.9
  80.2 1.8 collective-permute-done
  86.6 3.3 %multiply_reduce_fusion = (f32[256,8]{1,0:T(8,128)}, bf16[256,1,8,128]{3,2,0,1:T(8,128)(2,1)}) fusion(bf16[256,8,128]{2,1,0:T(8,128)(2,1)} %param.13, f32[256,8]{1,0:T(8,128)} %copy.79, f32[256,1,8,128]{3,0,2,1:T(8,128)S(1)} %get-tuple-element.648), kind=kLoop, calls=%fused_computation.83 | loop fusion | flops 1570816 | bytes 2113536 | tf_op jit(solution)/shard_map/reduce_sum | solution.py:127
  90.9 73.6 %while.49 = (s32[]{:T(128)}, bf16[256,1,128]{2,0,1:T(8,128)(2,1)S(1)}, bf16[256,1,128]{2,0,1:T(8,128)(2,1)S(1)}, f32[256,1,128]{2,0,1:T(8,128)S(1)}, f32[256,1,1...) while((s32[]{:T(128)}, ...), condition=%wide.region_12.13_spmd.clone, body=%wide.region_10.12_spmd.clone.sunk | while | flops 675742272 | bytes 16081516 | solution.py:149
  91.7 1.3 bitcast_select_fusion.4
  94.4 1.6 collective-permute-start.5
  96.8 2.6 %collective-permute-done.4 = bf16[256,1,128]{2,0,1:T(8,128)(2,1)S(1)} collective-permute-done((bf16[256,1,128]{2,0,1:T(8,128)(2,1)S(1)}, bf16[256,1,128]{2,0,1:T(8,128)(2,1)S(1)}, u32[]{:S(2)}, u32[]{:S(2)}) %collective-permute-start.4) | collective-permute-done | bytes 65568 | tf_op jit(solution)/shard_map/while/body/eval_jaxpr/ppermute | solution.py:17
  100.9 1.3 bitcast_select_fusion.4
  103.6 1.6 collective-permute-start.5
  106.0 2.6 %collective-permute-done.4 = bf16[256,1,128]{2,0,1:T(8,128)(2,1)S(1)} collective-permute-done((bf16[256,1,128]{2,0,1:T(8,128)(2,1)S(1)}, bf16[256,1,128]{2,0,1:T(8,128)(2,1)S(1)}, u32[]{:S(2)}, u32[]{:S(2)}) %collective-permute-start.4) | collective-permute-done | bytes 65568 | tf_op jit(solution)/shard_map/while/body/eval_jaxpr/ppermute | solution.py:17
  112.8 1.5 collective-permute-start.5
  115.2 2.6 %collective-permute-done.4 = bf16[256,1,128]{2,0,1:T(8,128)(2,1)S(1)} collective-permute-done((bf16[256,1,128]{2,0,1:T(8,128)(2,1)S(1)}, bf16[256,1,128]{2,0,1:T(8,128)(2,1)S(1)}, u32[]{:S(2)}, u32[]{:S(2)}) %collective-permute-start.4) | collective-permute-done | bytes 65568 | tf_op jit(solution)/shard_map/while/body/eval_jaxpr/ppermute | solution.py:17
  119.3 1.3 bitcast_select_fusion.4
  122.0 1.5 collective-permute-start.5
  124.4 2.6 %collective-permute-done.4 = bf16[256,1,128]{2,0,1:T(8,128)(2,1)S(1)} collective-permute-done((bf16[256,1,128]{2,0,1:T(8,128)(2,1)S(1)}, bf16[256,1,128]{2,0,1:T(8,128)(2,1)S(1)}, u32[]{:S(2)}, u32[]{:S(2)}) %collective-permute-start.4) | collective-permute-done | bytes 65568 | tf_op jit(solution)/shard_map/while/body/eval_jaxpr/ppermute | solution.py:17
  128.5 1.3 bitcast_select_fusion.4
  131.2 1.5 collective-permute-start.5
  133.6 2.6 %collective-permute-done.4 = bf16[256,1,128]{2,0,1:T(8,128)(2,1)S(1)} collective-permute-done((bf16[256,1,128]{2,0,1:T(8,128)(2,1)S(1)}, bf16[256,1,128]{2,0,1:T(8,128)(2,1)S(1)}, u32[]{:S(2)}, u32[]{:S(2)}) %collective-permute-start.4) | collective-permute-done | bytes 65568 | tf_op jit(solution)/shard_map/while/body/eval_jaxpr/ppermute | solution.py:17
  137.7 1.3 bitcast_select_fusion.4
  140.4 1.5 collective-permute-start.5
  142.8 2.6 %collective-permute-done.4 = bf16[256,1,128]{2,0,1:T(8,128)(2,1)S(1)} collective-permute-done((bf16[256,1,128]{2,0,1:T(8,128)(2,1)S(1)}, bf16[256,1,128]{2,0,1:T(8,128)(2,1)S(1)}, u32[]{:S(2)}, u32[]{:S(2)}) %collective-permute-start.4) | collective-permute-done | bytes 65568 | tf_op jit(solution)/shard_map/while/body/eval_jaxpr/ppermute | solution.py:17
  149.6 1.5 collective-permute-start.5
  152.0 2.6 %collective-permute-done.4 = bf16[256,1,128]{2,0,1:T(8,128)(2,1)S(1)} collective-permute-done((bf16[256,1,128]{2,0,1:T(8,128)(2,1)S(1)}, bf16[256,1,128]{2,0,1:T(8,128)(2,1)S(1)}, u32[]{:S(2)}, u32[]{:S(2)}) %collective-permute-start.4) | collective-permute-done | bytes 65568 | tf_op jit(solution)/shard_map/while/body/eval_jaxpr/ppermute | solution.py:17
  158.8 1.5 collective-permute-start.5
  161.2 2.6 %collective-permute-done.4 = bf16[256,1,128]{2,0,1:T(8,128)(2,1)S(1)} collective-permute-done((bf16[256,1,128]{2,0,1:T(8,128)(2,1)S(1)}, bf16[256,1,128]{2,0,1:T(8,128)(2,1)S(1)}, u32[]{:S(2)}, u32[]{:S(2)}) %collective-permute-start.4) | collective-permute-done | bytes 65568 | tf_op jit(solution)/shard_map/while/body/eval_jaxpr/ppermute | solution.py:17
  166.4 3.3 %all-to-all-start.2 = ((bf16[4,2,4096]{2,1,0:T(2,128)(2,1)}), bf16[4,2,4096]{2,1,0:T(2,128)(2,1)S(1)}, u32[]{:S(2)}, u32[]{:S(2)}) async-start(bf16[4,2,4096]{2,1,0:T(2,128)(2,1)} %reshape.646), calls=%async_computation.2 | async-start | bytes 131072 | tf_op jit(solution)/shard_map/all_to_all | solution.py:162
  171.1 3.5 %all-to-all-done.2 = bf16[4,2,4096]{2,1,0:T(2,128)(2,1)S(1)} async-done(((bf16[4,2,4096]{2,1,0:T(2,128)(2,1)}), bf16[4,2,4096]{2,1,0:T(2,128)(2,1)S(1)}, u32[]{:S(2)}, u32[]{:S(2)}) %all-to-all-start.2) | async-done | bytes 65568 | tf_op jit(solution)/shard_map/all_to_all | solution.py:162
  174.5 3.3 %all-to-all-start.3 = ((bf16[4,2,4096]{2,1,0:T(2,128)(2,1)}), bf16[4,2,4096]{2,1,0:T(2,128)(2,1)S(1)}, u32[]{:S(2)}, u32[]{:S(2)}) async-start(bf16[4,2,4096]{2,1,0:T(2,128)(2,1)} %reshape.648), calls=%async_computation.3 | async-start | bytes 131072 | tf_op jit(solution)/shard_map/all_to_all | solution.py:163
  177.8 1.5 fusion.61
  180.1 2.6 %all-to-all-done.3 = bf16[4,2,4096]{2,1,0:T(2,128)(2,1)S(1)} async-done(((bf16[4,2,4096]{2,1,0:T(2,128)(2,1)}), bf16[4,2,4096]{2,1,0:T(2,128)(2,1)S(1)}, u32[]{:S(2)}, u32[]{:S(2)}) %all-to-all-start.3) | async-done | bytes 65568 | tf_op jit(solution)/shard_map/all_to_all | solution.py:163
  (318 shorter events, 89.7 us)
Async XLA Ops:
  2.2 10.0 %all-to-all-start = ((bf16[64,4,128]{2,0,1:T(8,128)(2,1)}), bf16[64,4,128]{2,0,1:T(8,128)(2,1)S(1)}, u32[]{:S(2)}, u32[]{:S(2)}) async-start(bf16[64,4,128]{2,0,1:T(8,128)(2,1)} %copy.74), calls=%async_computation | async-start | bytes 131072 | tf_op jit(solution)/shard_map/all_to_all | solution.py:76
  12.2 8.1 %all-to-all-start.1 = ((bf16[64,4,128]{2,0,1:T(8,128)(2,1)}), bf16[64,4,128]{2,0,1:T(8,128)(2,1)S(1)}, u32[]{:S(2)}, u32[]{:S(2)}) async-start(bf16[64,4,128]{2,0,1:T(8,128)(2,1)} %copy.75), calls=%async_computation.1 | async-start | bytes 131072 | tf_op jit(solution)/shard_map/all_to_all | solution.py:77
  22.9 5.8 %collective-permute-start = (bf16[256,1,128]{2,0,1:T(8,128)(2,1)}, bf16[256,1,128]{2,0,1:T(8,128)(2,1)S(1)}, u32[]{:S(2)}, u32[]{:S(2)}) collective-permute-start(bf16[256,1,128]{2,0,1:T(8,128)(2,1)} %get-tuple-element.1124), channel_id=1, source_target_pairs={{0,4},{4,8},{8,12},{12,16},{16,20},{20,24},{24,28},{28,0},{1,5},{5... | collective-permute-start | bytes 196616 | tf_op jit(solution)/shard_map/while/body/eval_jaxpr/ppermute | solution.py:17
  22.9 7.3 %collective-permute-start.1 = (bf16[256,1,128]{2,0,1:T(8,128)(2,1)}, bf16[256,1,128]{2,0,1:T(8,128)(2,1)S(1)}, u32[]{:S(2)}, u32[]{:S(2)}) collective-permute-start(bf16[256,1,128]{2,0,1:T(8,128)(2,1)} %get-tuple-element.1125), channel_id=1, source_target_pairs={{0,4},{4,8},{8,12},{12,16},{16,20},{20,24},{24,28},{28,0},{1,5},{5... | collective-permute-start | bytes 196616 | tf_op jit(solution)/shard_map/while/body/eval_jaxpr/ppermute | solution.py:17
  31.8 5.8 %collective-permute-start = (bf16[256,1,128]{2,0,1:T(8,128)(2,1)}, bf16[256,1,128]{2,0,1:T(8,128)(2,1)S(1)}, u32[]{:S(2)}, u32[]{:S(2)}) collective-permute-start(bf16[256,1,128]{2,0,1:T(8,128)(2,1)} %get-tuple-element.1124), channel_id=1, source_target_pairs={{0,4},{4,8},{8,12},{12,16},{16,20},{20,24},{24,28},{28,0},{1,5},{5... | collective-permute-start | bytes 196616 | tf_op jit(solution)/shard_map/while/body/eval_jaxpr/ppermute | solution.py:17
  31.8 7.3 %collective-permute-start.1 = (bf16[256,1,128]{2,0,1:T(8,128)(2,1)}, bf16[256,1,128]{2,0,1:T(8,128)(2,1)S(1)}, u32[]{:S(2)}, u32[]{:S(2)}) collective-permute-start(bf16[256,1,128]{2,0,1:T(8,128)(2,1)} %get-tuple-element.1125), channel_id=1, source_target_pairs={{0,4},{4,8},{8,12},{12,16},{16,20},{20,24},{24,28},{28,0},{1,5},{5... | collective-permute-start | bytes 196616 | tf_op jit(solution)/shard_map/while/body/eval_jaxpr/ppermute | solution.py:17
  40.7 5.8 %collective-permute-start = (bf16[256,1,128]{2,0,1:T(8,128)(2,1)}, bf16[256,1,128]{2,0,1:T(8,128)(2,1)S(1)}, u32[]{:S(2)}, u32[]{:S(2)}) collective-permute-start(bf16[256,1,128]{2,0,1:T(8,128)(2,1)} %get-tuple-element.1124), channel_id=1, source_target_pairs={{0,4},{4,8},{8,12},{12,16},{16,20},{20,24},{24,28},{28,0},{1,5},{5... | collective-permute-start | bytes 196616 | tf_op jit(solution)/shard_map/while/body/eval_jaxpr/ppermute | solution.py:17
  40.7 7.3 %collective-permute-start.1 = (bf16[256,1,128]{2,0,1:T(8,128)(2,1)}, bf16[256,1,128]{2,0,1:T(8,128)(2,1)S(1)}, u32[]{:S(2)}, u32[]{:S(2)}) collective-permute-start(bf16[256,1,128]{2,0,1:T(8,128)(2,1)} %get-tuple-element.1125), channel_id=1, source_target_pairs={{0,4},{4,8},{8,12},{12,16},{16,20},{20,24},{24,28},{28,0},{1,5},{5... | collective-permute-start | bytes 196616 | tf_op jit(solution)/shard_map/while/body/eval_jaxpr/ppermute | solution.py:17
  49.6 5.8 %collective-permute-start = (bf16[256,1,128]{2,0,1:T(8,128)(2,1)}, bf16[256,1,128]{2,0,1:T(8,128)(2,1)S(1)}, u32[]{:S(2)}, u32[]{:S(2)}) collective-permute-start(bf16[256,1,128]{2,0,1:T(8,128)(2,1)} %get-tuple-element.1124), channel_id=1, source_target_pairs={{0,4},{4,8},{8,12},{12,16},{16,20},{20,24},{24,28},{28,0},{1,5},{5... | collective-permute-start | bytes 196616 | tf_op jit(solution)/shard_map/while/body/eval_jaxpr/ppermute | solution.py:17
  49.6 7.3 %collective-permute-start.1 = (bf16[256,1,128]{2,0,1:T(8,128)(2,1)}, bf16[256,1,128]{2,0,1:T(8,128)(2,1)S(1)}, u32[]{:S(2)}, u32[]{:S(2)}) collective-permute-start(bf16[256,1,128]{2,0,1:T(8,128)(2,1)} %get-tuple-element.1125), channel_id=1, source_target_pairs={{0,4},{4,8},{8,12},{12,16},{16,20},{20,24},{24,28},{28,0},{1,5},{5... | collective-permute-start | bytes 196616 | tf_op jit(solution)/shard_map/while/body/eval_jaxpr/ppermute | solution.py:17
  58.5 5.8 %collective-permute-start = (bf16[256,1,128]{2,0,1:T(8,128)(2,1)}, bf16[256,1,128]{2,0,1:T(8,128)(2,1)S(1)}, u32[]{:S(2)}, u32[]{:S(2)}) collective-permute-start(bf16[256,1,128]{2,0,1:T(8,128)(2,1)} %get-tuple-element.1124), channel_id=1, source_target_pairs={{0,4},{4,8},{8,12},{12,16},{16,20},{20,24},{24,28},{28,0},{1,5},{5... | collective-permute-start | bytes 196616 | tf_op jit(solution)/shard_map/while/body/eval_jaxpr/ppermute | solution.py:17
  58.5 7.3 %collective-permute-start.1 = (bf16[256,1,128]{2,0,1:T(8,128)(2,1)}, bf16[256,1,128]{2,0,1:T(8,128)(2,1)S(1)}, u32[]{:S(2)}, u32[]{:S(2)}) collective-permute-start(bf16[256,1,128]{2,0,1:T(8,128)(2,1)} %get-tuple-element.1125), channel_id=1, source_target_pairs={{0,4},{4,8},{8,12},{12,16},{16,20},{20,24},{24,28},{28,0},{1,5},{5... | collective-permute-start | bytes 196616 | tf_op jit(solution)/shard_map/while/body/eval_jaxpr/ppermute | solution.py:17
  67.4 5.8 %collective-permute-start = (bf16[256,1,128]{2,0,1:T(8,128)(2,1)}, bf16[256,1,128]{2,0,1:T(8,128)(2,1)S(1)}, u32[]{:S(2)}, u32[]{:S(2)}) collective-permute-start(bf16[256,1,128]{2,0,1:T(8,128)(2,1)} %get-tuple-element.1124), channel_id=1, source_target_pairs={{0,4},{4,8},{8,12},{12,16},{16,20},{20,24},{24,28},{28,0},{1,5},{5... | collective-permute-start | bytes 196616 | tf_op jit(solution)/shard_map/while/body/eval_jaxpr/ppermute | solution.py:17
  67.4 7.3 %collective-permute-start.1 = (bf16[256,1,128]{2,0,1:T(8,128)(2,1)}, bf16[256,1,128]{2,0,1:T(8,128)(2,1)S(1)}, u32[]{:S(2)}, u32[]{:S(2)}) collective-permute-start(bf16[256,1,128]{2,0,1:T(8,128)(2,1)} %get-tuple-element.1125), channel_id=1, source_target_pairs={{0,4},{4,8},{8,12},{12,16},{16,20},{20,24},{24,28},{28,0},{1,5},{5... | collective-permute-start | bytes 196616 | tf_op jit(solution)/shard_map/while/body/eval_jaxpr/ppermute | solution.py:17
  76.3 5.8 %collective-permute-start = (bf16[256,1,128]{2,0,1:T(8,128)(2,1)}, bf16[256,1,128]{2,0,1:T(8,128)(2,1)S(1)}, u32[]{:S(2)}, u32[]{:S(2)}) collective-permute-start(bf16[256,1,128]{2,0,1:T(8,128)(2,1)} %get-tuple-element.1124), channel_id=1, source_target_pairs={{0,4},{4,8},{8,12},{12,16},{16,20},{20,24},{24,28},{28,0},{1,5},{5... | collective-permute-start | bytes 196616 | tf_op jit(solution)/shard_map/while/body/eval_jaxpr/ppermute | solution.py:17
  76.3 7.3 %collective-permute-start.1 = (bf16[256,1,128]{2,0,1:T(8,128)(2,1)}, bf16[256,1,128]{2,0,1:T(8,128)(2,1)S(1)}, u32[]{:S(2)}, u32[]{:S(2)}) collective-permute-start(bf16[256,1,128]{2,0,1:T(8,128)(2,1)} %get-tuple-element.1125), channel_id=1, source_target_pairs={{0,4},{4,8},{8,12},{12,16},{16,20},{20,24},{24,28},{28,0},{1,5},{5... | collective-permute-start | bytes 196616 | tf_op jit(solution)/shard_map/while/body/eval_jaxpr/ppermute | solution.py:17
  91.0 9.2 %collective-permute-start.2 = (bf16[256,1,128]{2,0,1:T(8,128)(2,1)S(1)}, bf16[256,1,128]{2,0,1:T(8,128)(2,1)S(1)}, u32[]{:S(2)}, u32[]{:S(2)}) collective-permute-start(bf16[256,1,128]{2,0,1:T(8,128)(2,1)S(1)} %copy.135), channel_id=1, source_target_pairs={{0,4},{4,8},{8,12},{12,16},{16,20},{20,24},{24,28},{28,0},{1,5},{5... | collective-permute-start | bytes 196616 | tf_op jit(solution)/shard_map/while/body/eval_jaxpr/ppermute | solution.py:17
  91.0 9.1 %collective-permute-start.3 = (bf16[256,1,128]{2,0,1:T(8,128)(2,1)S(1)}, bf16[256,1,128]{2,0,1:T(8,128)(2,1)S(1)}, u32[]{:S(2)}, u32[]{:S(2)}) collective-permute-start(bf16[256,1,128]{2,0,1:T(8,128)(2,1)S(1)} %copy.136), channel_id=1, source_target_pairs={{0,4},{4,8},{8,12},{12,16},{16,20},{20,24},{24,28},{28,0},{1,5},{5... | collective-permute-start | bytes 196616 | tf_op jit(solution)/shard_map/while/body/eval_jaxpr/ppermute | solution.py:17
  93.9 5.5 %collective-permute-start.4 = (bf16[256,1,128]{2,0,1:T(8,128)(2,1)S(1)}, bf16[256,1,128]{2,0,1:T(8,128)(2,1)S(1)}, u32[]{:S(2)}, u32[]{:S(2)}) collective-permute-start(bf16[256,1,128]{2,0,1:T(8,128)(2,1)S(1)} %fusion.114), channel_id=1, source_target_pairs={{0,4},{4,8},{8,12},{12,16},{16,20},{20,24},{24,28},{28,0},{1,5},{5... | collective-permute-start | bytes 196616 | tf_op jit(solution)/shard_map/while/body/eval_jaxpr/ppermute | solution.py:17
  94.4 5.7 %collective-permute-start.5 = (bf16[256,1,128]{2,0,1:T(8,128)(2,1)S(1)}, bf16[256,1,128]{2,0,1:T(8,128)(2,1)S(1)}, u32[]{:S(2)}, u32[]{:S(2)}) collective-permute-start(bf16[256,1,128]{2,0,1:T(8,128)(2,1)S(1)} %fusion.115), channel_id=1, source_target_pairs={{0,4},{4,8},{8,12},{12,16},{16,20},{20,24},{24,28},{28,0},{1,5},{5... | collective-permute-start | bytes 196616 | tf_op jit(solution)/shard_map/while/body/eval_jaxpr/ppermute | solution.py:17
  100.2 9.2 %collective-permute-start.2 = (bf16[256,1,128]{2,0,1:T(8,128)(2,1)S(1)}, bf16[256,1,128]{2,0,1:T(8,128)(2,1)S(1)}, u32[]{:S(2)}, u32[]{:S(2)}) collective-permute-start(bf16[256,1,128]{2,0,1:T(8,128)(2,1)S(1)} %copy.135), channel_id=1, source_target_pairs={{0,4},{4,8},{8,12},{12,16},{16,20},{20,24},{24,28},{28,0},{1,5},{5... | collective-permute-start | bytes 196616 | tf_op jit(solution)/shard_map/while/body/eval_jaxpr/ppermute | solution.py:17
  100.3 9.1 %collective-permute-start.3 = (bf16[256,1,128]{2,0,1:T(8,128)(2,1)S(1)}, bf16[256,1,128]{2,0,1:T(8,128)(2,1)S(1)}, u32[]{:S(2)}, u32[]{:S(2)}) collective-permute-start(bf16[256,1,128]{2,0,1:T(8,128)(2,1)S(1)} %copy.136), channel_id=1, source_target_pairs={{0,4},{4,8},{8,12},{12,16},{16,20},{20,24},{24,28},{28,0},{1,5},{5... | collective-permute-start | bytes 196616 | tf_op jit(solution)/shard_map/while/body/eval_jaxpr/ppermute | solution.py:17
  103.1 5.5 %collective-permute-start.4 = (bf16[256,1,128]{2,0,1:T(8,128)(2,1)S(1)}, bf16[256,1,128]{2,0,1:T(8,128)(2,1)S(1)}, u32[]{:S(2)}, u32[]{:S(2)}) collective-permute-start(bf16[256,1,128]{2,0,1:T(8,128)(2,1)S(1)} %fusion.114), channel_id=1, source_target_pairs={{0,4},{4,8},{8,12},{12,16},{16,20},{20,24},{24,28},{28,0},{1,5},{5... | collective-permute-start | bytes 196616 | tf_op jit(solution)/shard_map/while/body/eval_jaxpr/ppermute | solution.py:17
  103.6 5.7 %collective-permute-start.5 = (bf16[256,1,128]{2,0,1:T(8,128)(2,1)S(1)}, bf16[256,1,128]{2,0,1:T(8,128)(2,1)S(1)}, u32[]{:S(2)}, u32[]{:S(2)}) collective-permute-start(bf16[256,1,128]{2,0,1:T(8,128)(2,1)S(1)} %fusion.115), channel_id=1, source_target_pairs={{0,4},{4,8},{8,12},{12,16},{16,20},{20,24},{24,28},{28,0},{1,5},{5... | collective-permute-start | bytes 196616 | tf_op jit(solution)/shard_map/while/body/eval_jaxpr/ppermute | solution.py:17
  109.4 9.2 %collective-permute-start.2 = (bf16[256,1,128]{2,0,1:T(8,128)(2,1)S(1)}, bf16[256,1,128]{2,0,1:T(8,128)(2,1)S(1)}, u32[]{:S(2)}, u32[]{:S(2)}) collective-permute-start(bf16[256,1,128]{2,0,1:T(8,128)(2,1)S(1)} %copy.135), channel_id=1, source_target_pairs={{0,4},{4,8},{8,12},{12,16},{16,20},{20,24},{24,28},{28,0},{1,5},{5... | collective-permute-start | bytes 196616 | tf_op jit(solution)/shard_map/while/body/eval_jaxpr/ppermute | solution.py:17
  109.5 9.1 %collective-permute-start.3 = (bf16[256,1,128]{2,0,1:T(8,128)(2,1)S(1)}, bf16[256,1,128]{2,0,1:T(8,128)(2,1)S(1)}, u32[]{:S(2)}, u32[]{:S(2)}) collective-permute-start(bf16[256,1,128]{2,0,1:T(8,128)(2,1)S(1)} %copy.136), channel_id=1, source_target_pairs={{0,4},{4,8},{8,12},{12,16},{16,20},{20,24},{24,28},{28,0},{1,5},{5... | collective-permute-start | bytes 196616 | tf_op jit(solution)/shard_map/while/body/eval_jaxpr/ppermute | solution.py:17
  112.3 5.5 %collective-permute-start.4 = (bf16[256,1,128]{2,0,1:T(8,128)(2,1)S(1)}, bf16[256,1,128]{2,0,1:T(8,128)(2,1)S(1)}, u32[]{:S(2)}, u32[]{:S(2)}) collective-permute-start(bf16[256,1,128]{2,0,1:T(8,128)(2,1)S(1)} %fusion.114), channel_id=1, source_target_pairs={{0,4},{4,8},{8,12},{12,16},{16,20},{20,24},{24,28},{28,0},{1,5},{5... | collective-permute-start | bytes 196616 | tf_op jit(solution)/shard_map/while/body/eval_jaxpr/ppermute | solution.py:17
  112.8 5.7 %collective-permute-start.5 = (bf16[256,1,128]{2,0,1:T(8,128)(2,1)S(1)}, bf16[256,1,128]{2,0,1:T(8,128)(2,1)S(1)}, u32[]{:S(2)}, u32[]{:S(2)}) collective-permute-start(bf16[256,1,128]{2,0,1:T(8,128)(2,1)S(1)} %fusion.115), channel_id=1, source_target_pairs={{0,4},{4,8},{8,12},{12,16},{16,20},{20,24},{24,28},{28,0},{1,5},{5... | collective-permute-start | bytes 196616 | tf_op jit(solution)/shard_map/while/body/eval_jaxpr/ppermute | solution.py:17
  118.6 9.2 %collective-permute-start.2 = (bf16[256,1,128]{2,0,1:T(8,128)(2,1)S(1)}, bf16[256,1,128]{2,0,1:T(8,128)(2,1)S(1)}, u32[]{:S(2)}, u32[]{:S(2)}) collective-permute-start(bf16[256,1,128]{2,0,1:T(8,128)(2,1)S(1)} %copy.135), channel_id=1, source_target_pairs={{0,4},{4,8},{8,12},{12,16},{16,20},{20,24},{24,28},{28,0},{1,5},{5... | collective-permute-start | bytes 196616 | tf_op jit(solution)/shard_map/while/body/eval_jaxpr/ppermute | solution.py:17
  118.7 9.1 %collective-permute-start.3 = (bf16[256,1,128]{2,0,1:T(8,128)(2,1)S(1)}, bf16[256,1,128]{2,0,1:T(8,128)(2,1)S(1)}, u32[]{:S(2)}, u32[]{:S(2)}) collective-permute-start(bf16[256,1,128]{2,0,1:T(8,128)(2,1)S(1)} %copy.136), channel_id=1, source_target_pairs={{0,4},{4,8},{8,12},{12,16},{16,20},{20,24},{24,28},{28,0},{1,5},{5... | collective-permute-start | bytes 196616 | tf_op jit(solution)/shard_map/while/body/eval_jaxpr/ppermute | solution.py:17
  121.5 5.5 %collective-permute-start.4 = (bf16[256,1,128]{2,0,1:T(8,128)(2,1)S(1)}, bf16[256,1,128]{2,0,1:T(8,128)(2,1)S(1)}, u32[]{:S(2)}, u32[]{:S(2)}) collective-permute-start(bf16[256,1,128]{2,0,1:T(8,128)(2,1)S(1)} %fusion.114), channel_id=1, source_target_pairs={{0,4},{4,8},{8,12},{12,16},{16,20},{20,24},{24,28},{28,0},{1,5},{5... | collective-permute-start | bytes 196616 | tf_op jit(solution)/shard_map/while/body/eval_jaxpr/ppermute | solution.py:17
  122.0 5.7 %collective-permute-start.5 = (bf16[256,1,128]{2,0,1:T(8,128)(2,1)S(1)}, bf16[256,1,128]{2,0,1:T(8,128)(2,1)S(1)}, u32[]{:S(2)}, u32[]{:S(2)}) collective-permute-start(bf16[256,1,128]{2,0,1:T(8,128)(2,1)S(1)} %fusion.115), channel_id=1, source_target_pairs={{0,4},{4,8},{8,12},{12,16},{16,20},{20,24},{24,28},{28,0},{1,5},{5... | collective-permute-start | bytes 196616 | tf_op jit(solution)/shard_map/while/body/eval_jaxpr/ppermute | solution.py:17
  127.8 9.2 %collective-permute-start.2 = (bf16[256,1,128]{2,0,1:T(8,128)(2,1)S(1)}, bf16[256,1,128]{2,0,1:T(8,128)(2,1)S(1)}, u32[]{:S(2)}, u32[]{:S(2)}) collective-permute-start(bf16[256,1,128]{2,0,1:T(8,128)(2,1)S(1)} %copy.135), channel_id=1, source_target_pairs={{0,4},{4,8},{8,12},{12,16},{16,20},{20,24},{24,28},{28,0},{1,5},{5... | collective-permute-start | bytes 196616 | tf_op jit(solution)/shard_map/while/body/eval_jaxpr/ppermute | solution.py:17
  127.9 9.1 %collective-permute-start.3 = (bf16[256,1,128]{2,0,1:T(8,128)(2,1)S(1)}, bf16[256,1,128]{2,0,1:T(8,128)(2,1)S(1)}, u32[]{:S(2)}, u32[]{:S(2)}) collective-permute-start(bf16[256,1,128]{2,0,1:T(8,128)(2,1)S(1)} %copy.136), channel_id=1, source_target_pairs={{0,4},{4,8},{8,12},{12,16},{16,20},{20,24},{24,28},{28,0},{1,5},{5... | collective-permute-start | bytes 196616 | tf_op jit(solution)/shard_map/while/body/eval_jaxpr/ppermute | solution.py:17
  131.2 5.7 %collective-permute-start.5 = (bf16[256,1,128]{2,0,1:T(8,128)(2,1)S(1)}, bf16[256,1,128]{2,0,1:T(8,128)(2,1)S(1)}, u32[]{:S(2)}, u32[]{:S(2)}) collective-permute-start(bf16[256,1,128]{2,0,1:T(8,128)(2,1)S(1)} %fusion.115), channel_id=1, source_target_pairs={{0,4},{4,8},{8,12},{12,16},{16,20},{20,24},{24,28},{28,0},{1,5},{5... | collective-permute-start | bytes 196616 | tf_op jit(solution)/shard_map/while/body/eval_jaxpr/ppermute | solution.py:17
  137.0 9.2 %collective-permute-start.2 = (bf16[256,1,128]{2,0,1:T(8,128)(2,1)S(1)}, bf16[256,1,128]{2,0,1:T(8,128)(2,1)S(1)}, u32[]{:S(2)}, u32[]{:S(2)}) collective-permute-start(bf16[256,1,128]{2,0,1:T(8,128)(2,1)S(1)} %copy.135), channel_id=1, source_target_pairs={{0,4},{4,8},{8,12},{12,16},{16,20},{20,24},{24,28},{28,0},{1,5},{5... | collective-permute-start | bytes 196616 | tf_op jit(solution)/shard_map/while/body/eval_jaxpr/ppermute | solution.py:17
  137.1 9.1 %collective-permute-start.3 = (bf16[256,1,128]{2,0,1:T(8,128)(2,1)S(1)}, bf16[256,1,128]{2,0,1:T(8,128)(2,1)S(1)}, u32[]{:S(2)}, u32[]{:S(2)}) collective-permute-start(bf16[256,1,128]{2,0,1:T(8,128)(2,1)S(1)} %copy.136), channel_id=1, source_target_pairs={{0,4},{4,8},{8,12},{12,16},{16,20},{20,24},{24,28},{28,0},{1,5},{5... | collective-permute-start | bytes 196616 | tf_op jit(solution)/shard_map/while/body/eval_jaxpr/ppermute | solution.py:17
  139.9 5.5 %collective-permute-start.4 = (bf16[256,1,128]{2,0,1:T(8,128)(2,1)S(1)}, bf16[256,1,128]{2,0,1:T(8,128)(2,1)S(1)}, u32[]{:S(2)}, u32[]{:S(2)}) collective-permute-start(bf16[256,1,128]{2,0,1:T(8,128)(2,1)S(1)} %fusion.114), channel_id=1, source_target_pairs={{0,4},{4,8},{8,12},{12,16},{16,20},{20,24},{24,28},{28,0},{1,5},{5... | collective-permute-start | bytes 196616 | tf_op jit(solution)/shard_map/while/body/eval_jaxpr/ppermute | solution.py:17
  140.4 5.7 %collective-permute-start.5 = (bf16[256,1,128]{2,0,1:T(8,128)(2,1)S(1)}, bf16[256,1,128]{2,0,1:T(8,128)(2,1)S(1)}, u32[]{:S(2)}, u32[]{:S(2)}) collective-permute-start(bf16[256,1,128]{2,0,1:T(8,128)(2,1)S(1)} %fusion.115), channel_id=1, source_target_pairs={{0,4},{4,8},{8,12},{12,16},{16,20},{20,24},{24,28},{28,0},{1,5},{5... | collective-permute-start | bytes 196616 | tf_op jit(solution)/shard_map/while/body/eval_jaxpr/ppermute | solution.py:17
  146.2 9.2 %collective-permute-start.2 = (bf16[256,1,128]{2,0,1:T(8,128)(2,1)S(1)}, bf16[256,1,128]{2,0,1:T(8,128)(2,1)S(1)}, u32[]{:S(2)}, u32[]{:S(2)}) collective-permute-start(bf16[256,1,128]{2,0,1:T(8,128)(2,1)S(1)} %copy.135), channel_id=1, source_target_pairs={{0,4},{4,8},{8,12},{12,16},{16,20},{20,24},{24,28},{28,0},{1,5},{5... | collective-permute-start | bytes 196616 | tf_op jit(solution)/shard_map/while/body/eval_jaxpr/ppermute | solution.py:17
  146.3 9.1 %collective-permute-start.3 = (bf16[256,1,128]{2,0,1:T(8,128)(2,1)S(1)}, bf16[256,1,128]{2,0,1:T(8,128)(2,1)S(1)}, u32[]{:S(2)}, u32[]{:S(2)}) collective-permute-start(bf16[256,1,128]{2,0,1:T(8,128)(2,1)S(1)} %copy.136), channel_id=1, source_target_pairs={{0,4},{4,8},{8,12},{12,16},{16,20},{20,24},{24,28},{28,0},{1,5},{5... | collective-permute-start | bytes 196616 | tf_op jit(solution)/shard_map/while/body/eval_jaxpr/ppermute | solution.py:17
  149.6 5.7 %collective-permute-start.5 = (bf16[256,1,128]{2,0,1:T(8,128)(2,1)S(1)}, bf16[256,1,128]{2,0,1:T(8,128)(2,1)S(1)}, u32[]{:S(2)}, u32[]{:S(2)}) collective-permute-start(bf16[256,1,128]{2,0,1:T(8,128)(2,1)S(1)} %fusion.115), channel_id=1, source_target_pairs={{0,4},{4,8},{8,12},{12,16},{16,20},{20,24},{24,28},{28,0},{1,5},{5... | collective-permute-start | bytes 196616 | tf_op jit(solution)/shard_map/while/body/eval_jaxpr/ppermute | solution.py:17
  155.4 9.2 %collective-permute-start.2 = (bf16[256,1,128]{2,0,1:T(8,128)(2,1)S(1)}, bf16[256,1,128]{2,0,1:T(8,128)(2,1)S(1)}, u32[]{:S(2)}, u32[]{:S(2)}) collective-permute-start(bf16[256,1,128]{2,0,1:T(8,128)(2,1)S(1)} %copy.135), channel_id=1, source_target_pairs={{0,4},{4,8},{8,12},{12,16},{16,20},{20,24},{24,28},{28,0},{1,5},{5... | collective-permute-start | bytes 196616 | tf_op jit(solution)/shard_map/while/body/eval_jaxpr/ppermute | solution.py:17
  155.5 9.1 %collective-permute-start.3 = (bf16[256,1,128]{2,0,1:T(8,128)(2,1)S(1)}, bf16[256,1,128]{2,0,1:T(8,128)(2,1)S(1)}, u32[]{:S(2)}, u32[]{:S(2)}) collective-permute-start(bf16[256,1,128]{2,0,1:T(8,128)(2,1)S(1)} %copy.136), channel_id=1, source_target_pairs={{0,4},{4,8},{8,12},{12,16},{16,20},{20,24},{24,28},{28,0},{1,5},{5... | collective-permute-start | bytes 196616 | tf_op jit(solution)/shard_map/while/body/eval_jaxpr/ppermute | solution.py:17
  158.3 5.5 %collective-permute-start.4 = (bf16[256,1,128]{2,0,1:T(8,128)(2,1)S(1)}, bf16[256,1,128]{2,0,1:T(8,128)(2,1)S(1)}, u32[]{:S(2)}, u32[]{:S(2)}) collective-permute-start(bf16[256,1,128]{2,0,1:T(8,128)(2,1)S(1)} %fusion.114), channel_id=1, source_target_pairs={{0,4},{4,8},{8,12},{12,16},{16,20},{20,24},{24,28},{28,0},{1,5},{5... | collective-permute-start | bytes 196616 | tf_op jit(solution)/shard_map/while/body/eval_jaxpr/ppermute | solution.py:17
  158.8 5.7 %collective-permute-start.5 = (bf16[256,1,128]{2,0,1:T(8,128)(2,1)S(1)}, bf16[256,1,128]{2,0,1:T(8,128)(2,1)S(1)}, u32[]{:S(2)}, u32[]{:S(2)}) collective-permute-start(bf16[256,1,128]{2,0,1:T(8,128)(2,1)S(1)} %fusion.115), channel_id=1, source_target_pairs={{0,4},{4,8},{8,12},{12,16},{16,20},{20,24},{24,28},{28,0},{1,5},{5... | collective-permute-start | bytes 196616 | tf_op jit(solution)/shard_map/while/body/eval_jaxpr/ppermute | solution.py:17
  166.4 8.1 %all-to-all-start.2 = ((bf16[4,2,4096]{2,1,0:T(2,128)(2,1)}), bf16[4,2,4096]{2,1,0:T(2,128)(2,1)S(1)}, u32[]{:S(2)}, u32[]{:S(2)}) async-start(bf16[4,2,4096]{2,1,0:T(2,128)(2,1)} %reshape.646), calls=%async_computation.2 | async-start | bytes 131072 | tf_op jit(solution)/shard_map/all_to_all | solution.py:162
  174.5 8.1 %all-to-all-start.3 = ((bf16[4,2,4096]{2,1,0:T(2,128)(2,1)}), bf16[4,2,4096]{2,1,0:T(2,128)(2,1)S(1)}, u32[]{:S(2)}, u32[]{:S(2)}) async-start(bf16[4,2,4096]{2,1,0:T(2,128)(2,1)} %reshape.648), calls=%async_computation.3 | async-start | bytes 131072 | tf_op jit(solution)/shard_map/all_to_all | solution.py:163
  (14 other events, 80.7 us)
where the time goes:
time: 185 us; the launch traced here: 183 us
  waiting for transfers between devices  43.8 us (24%)
  other arithmetic  43.5 us (24%)
  matrix products  38.5 us (21%)
  starting transfers between devices  33.8 us (18%)
  local copies, waits for them, and re-layouts  21 us (11%)
    ppermute x46, waiting for transfers between devices, from_behind(): return lax.ppermute(value, axis, pairs)  34.9 us
    ppermute x46, starting transfers between devices, from_behind(): return lax.ppermute(value, axis, pairs)  18.8 us
    dot_general x16, matrix products, block_scores(): jnp.einsum('tngd,knd->tngk', query_block, key_block, preferred_element_ty...  13.9 us
    unnamed x39, local copies, waits for them, and re-layouts  10.8 us
    le x15, other arithmetic, block_mask(): key_pos[None, :] <= query_pos[:, None]  9.68 us
    while x37, local copies, waits for them, and re-layouts  8.95 us
    reduce_sum x16, other arithmetic, row_info(): jnp.sum((shard_tiles[:, None] >= doc_ends[None, :]).astype(jnp.int32), ax...  7.69 us
    dot_general x8, matrix products, forward_block(): jnp.einsum('tngk,knd->tngd', weights.astype(jnp.bfloat16), value_block, p...  7.21 us
  transfers between devices with their start and end apart: 50, of which 27 were waited for; matrix products, arithmetic and copies ran while one was open for 43% of the time, Pallas kernels for 0%

commit v1 on v0

v1 whole, which is shorter than its diff:
```python
import functools
import math

import jax
import jax.numpy as jnp
from jax import lax
from jax.experimental import pallas as pl
from jax.experimental.pallas import tpu as pltpu
from jax.sharding import PartitionSpec as P

TILE = 128
NEG = -1e30
MESH = pl.DeviceIdType.MESH
VMEM_LIMIT = 48 * 1024 * 1024


def peers(n_ctx, n_head):
    ctx = lax.axis_index("ctx")
    head = lax.axis_index("head")
    core = lax.rem(ctx, 2)
    rail = lax.div(ctx, 2)
    n_rail = n_ctx // 2
    sibling = rail * 2 + (1 - core)
    return ctx, head, core, rail, n_rail, sibling


def entry_barrier(ctx, head, core, rail, n_rail, sibling, n_head):
    barrier = pltpu.get_barrier_semaphore()
    for d in range(1, n_head):
        pl.semaphore_signal(
            barrier, inc=1, device_id=(ctx, lax.rem(head + d, n_head)), device_id_type=MESH
        )
    for d in range(1, n_rail):
        pl.semaphore_signal(
            barrier,
            inc=1,
            device_id=(lax.rem(rail + d, n_rail) * 2 + core, head),
            device_id_type=MESH,
        )
    pl.semaphore_signal(barrier, inc=1, device_id=(sibling, head), device_id_type=MESH)
    pl.semaphore_wait(barrier, n_head - 1 + n_rail - 1 + 1)


def remote(src, dst, send, recv, ctx, head):
    return pltpu.make_async_remote_copy(
        src_ref=src,
        dst_ref=dst,
        send_sem=send,
        recv_sem=recv,
        device_id=(ctx, head),
        device_id_type=MESH,
    )


def gather_kernel(n_ctx, n_head, k_ref, v_ref, out_ref, turned, head_sems, rail_sems, sib_sems, fwd_sems):
    ctx, head, core, rail, n_rail, sibling = peers(n_ctx, n_head)
    for g in range(n_head):
        turned[g, 0] = k_ref[:, g * 128 : (g + 1) * 128]
        turned[g, 1] = v_ref[:, g * 128 : (g + 1) * 128]
    out_ref[:, ctx, head] = turned[head]
    entry_barrier(ctx, head, core, rail, n_rail, sibling, n_head)

    def head_copy(d):
        target = lax.rem(head + d, n_head)
        return remote(
            turned.at[target], out_ref.at[:, ctx, head], head_sems.at[0, d], head_sems.at[1, d], ctx, target
        )

    for d in range(1, n_head):
        head_copy(d).start()

    def rail_copy(dz, d):
        source = lax.rem(head + n_head - d, n_head)
        target = lax.rem(rail + dz, n_rail) * 2 + core
        block = out_ref.at[:, ctx, source]
        return remote(block, block, rail_sems.at[0, dz, d], rail_sems.at[1, dz, d], target, head)

    def sib_copy(d):
        source = lax.rem(head + n_head - d, n_head)
        block = out_ref.at[:, ctx, source]
        return remote(block, block, sib_sems.at[0, d], sib_sems.at[1, d], sibling, head)

    def fwd_copy(dz):
        block = out_ref.at[:, lax.rem(rail + n_rail - dz, n_rail) * 2 + core]
        return remote(block, block, fwd_sems.at[0, dz], fwd_sems.at[1, dz], sibling, head)

    for d in range(n_head):
        if d > 0:
            head_copy(d).wait_recv()
        for dz in range(1, n_rail):
            rail_copy(dz, d).start()
        sib_copy(d).start()
    for dz in range(1, n_rail):
        for d in range(n_head):
            rail_copy(dz, d).wait_recv()
        fwd_copy(dz).start()
    for d in range(1, n_head):
        head_copy(d).wait_send()
    for d in range(n_head):
        for dz in range(1, n_rail):
            rail_copy(dz, d).wait_send()
        sib_copy(d).wait()
    for dz in range(1, n_rail):
        fwd_copy(dz).wait()


def reduce_kernel(
    n_ctx, n_head, part_ref, k_ref, v_ref, sib_in, summed, rail_in, turned, head_in,
    sib_sems, rail_sems, head_sems,
):
    ctx, head, core, rail, n_rail, sibling = peers(n_ctx, n_head)
    entry_barrier(ctx, head, core, rail, n_rail, sibling, n_head)

    def rail_of(dz):
        return lax.rem(rail + dz, n_rail)

    def sib_copy(dz):
        return remote(
            part_ref.at[:, rail_of(dz) * 2 + (1 - core)],
            sib_in.at[dz],
            sib_sems.at[0, dz],
            sib_sems.at[1, dz],
            sibling,
            head,
        )

    def rail_copy(dz):
        return remote(
            summed.at[dz], rail_in.at[dz], rail_sems.at[0, dz], rail_sems.at[1, dz],
            rail_of(dz) * 2 + core, head,
        )

    def head_copy(d):
        target = lax.rem(head + d, n_head)
        return remote(
            turned.at[target], head_in.at[d], head_sems.at[0, d], head_sems.at[1, d], ctx, target
        )

    order = list(range(n_rail - 1, 0, -1)) + [0]
    for dz in order:
        sib_copy(dz).start()
    total = None
    for dz in order:
        sib_copy(dz).wait_recv()
        own = part_ref[:, rail_of(dz) * 2 + core].astype(jnp.float32)
        both = own + sib_in[dz].astype(jnp.float32)
        if dz > 0:
            summed[dz] = both.astype(jnp.bfloat16)
            rail_copy(dz).start()
        else:
            total = both
    for dz in range(1, n_rail):
        rail_copy(dz).wait_recv()
        total = total + rail_in[dz].astype(jnp.float32)
    scale = 1.0 / math.sqrt(128)
    for g in range(n_head):
        turned[g, 0] = (total[0, g] * scale).astype(jnp.bfloat16)
        turned[g, 1] = total[1, g].astype(jnp.bfloat16)
    for d in range(1, n_head):
        head_copy(d).start()
    head_in[0] = turned[head]
    for d in range(1, n_head):
        head_copy(d).wait_recv()
    for g in range(n_head):
        place = lax.rem(head - g + n_head, n_head)
        k_ref[:, g * 128 : (g + 1) * 128] = head_in[place, 0]
        v_ref[:, g * 128 : (g + 1) * 128] = head_in[place, 1]
    for dz in range(n_rail):
        sib_copy(dz).wait_send()
    for dz in range(1, n_rail):
        rail_copy(dz).wait_send()
    for d in range(1, n_head):
        head_copy(d).wait_send()


def dot(a, b):
    return jnp.dot(a, b, preferred_element_type=jnp.float32)


def attention_kernel(
    tiles, group, docs, order_ref, docs_ref, q_ref, g_ref, kv_ref, o_ref, dq_ref, dkv_ref,
    slot_of, k_t, v_t, q_t, g_t, g_s, g_st, scores, weights, o_t, dq_t, dkv, apart,
):
    step = pl.program_id(0)
    per_shard = pl.num_programs(0)
    rows = TILE * group
    scale = 1.0 / math.sqrt(128)

    @pl.when(step == 0)
    def _():
        for s in range(tiles):
            slot_of[order_ref[s]] = s

        @pl.loop(0, tiles)
        def _(s):
            k_t[s] = kv_ref[0, s].T
            v_t[s] = kv_ref[1, s].T

        dkv[...] = jnp.zeros_like(dkv)
        key = lax.broadcasted_iota(jnp.int32, (TILE, rows), 0)
        row = lax.broadcasted_iota(jnp.int32, (TILE, rows), 1)
        apart[...] = key - lax.div(row, group)

    mine = order_ref[lax.axis_index("ctx") * per_shard + step]
    end, first = 0, 0
    for d in range(docs):
        end = end + docs_ref[d]
        first = jnp.where(end <= mine, end, first)
    count = mine - first + 1
    turns = lax.div(count + 1, 2)

    q_t[...] = q_ref[...].T
    g_t[...] = g_ref[...].T

    def pair(j):
        near = slot_of[mine - 2 * j]
        far = slot_of[jnp.maximum(mine - 2 * j - 1, 0)]
        return near, far

    def cut(j):
        near_cut = jnp.where(j == 0, 0, TILE)
        far_cut = jnp.where(2 * j + 1 < count, TILE, -TILE)
        return near_cut, far_cut

    def top_turn(j, top):
        for half, (slot, limit) in enumerate(zip(pair(j), cut(j))):
            s = dot(kv_ref[0, slot], q_t[...])
            s = jnp.where(apart[...] <= limit, s, NEG)
            scores[j, half * TILE : (half + 1) * TILE] = s
            top = jnp.maximum(top, jnp.max(s.reshape(TILE // 8, 8, rows), axis=0))
        return top

    top = lax.fori_loop(0, turns, top_turn, jnp.full((8, rows), NEG, jnp.float32))
    top = jnp.max(top, axis=0, keepdims=True)

    o_t[...] = jnp.zeros_like(o_t)

    def sum_turn(j, total):
        slots = pair(j)
        w = jnp.exp((scores[j] - top) * scale)
        total = total + jnp.sum(w.reshape(2 * TILE // 8, 8, rows), axis=0)
        w = w.astype(jnp.bfloat16)
        weights[j] = w
        values = jnp.concatenate([v_t[slots[0]], v_t[slots[1]]], axis=1)
        o_t[...] += dot(values, w)
        return total

    total = lax.fori_loop(0, turns, sum_turn, jnp.zeros((8, rows), jnp.float32))
    inverse = 1.0 / jnp.sum(total, axis=0, keepdims=True)
    out_t = (o_t[...] * inverse).astype(jnp.bfloat16)
    o_ref[...] = out_t.T
    grads = g_t[...].astype(jnp.float32)
    delta = jnp.sum(grads * out_t.astype(jnp.float32), axis=0, keepdims=True) * inverse
    scaled = (grads * inverse).astype(jnp.bfloat16)
    g_st[...] = scaled
    g_s[...] = scaled.T
    dq_t[...] = jnp.zeros_like(dq_t)

    def grad_turn(j, _):
        slots = pair(j)
        parts = []
        for half, slot in enumerate(slots):
            w = weights[j, half * TILE : (half + 1) * TILE]
            dp = dot(kv_ref[1, slot], g_st[...])
            ds = (w.astype(jnp.float32) * (dp - delta)).astype(jnp.bfloat16)
            parts.append(ds)
            dkv[0, slot] += dot(ds, q_ref[...])
            dkv[1, slot] += dot(w, g_s[...])
        keys = jnp.concatenate([k_t[slots[0]], k_t[slots[1]]], axis=1)
        dq_t[...] += dot(keys, jnp.concatenate(parts, axis=0))
        return 0

    lax.fori_loop(0, turns, grad_turn, 0)
    dq_ref[...] = (dq_t[...] * scale).astype(jnp.bfloat16).T

    @pl.when(step == per_shard - 1)
    def _():
        dkv_ref[...] = dkv[...].astype(jnp.bfloat16)


def body(n_ctx, n_head, queries, key_proj, value_proj, out_grad, tile_order, doc_tiles):
    row_count, group, depth = queries.shape
    share, kv_heads, _ = key_proj.shape
    tiles = tile_order.shape[0]
    docs = doc_tiles.shape[0]
    n_rail = n_ctx // 2
    bf16, f32 = jnp.bfloat16, jnp.float32
    vmem = pl.BlockSpec(memory_space=pltpu.VMEM)
    dma = pltpu.SemaphoreType.DMA

    rows_kv = pl.pallas_call(
        functools.partial(gather_kernel, n_ctx, n_head),
        out_shape=jax.ShapeDtypeStruct((2, n_ctx, n_head, share, depth), bf16),
        in_specs=[vmem, vmem],
        out_specs=vmem,
        scratch_shapes=[
            pltpu.VMEM((n_head, 2, share, depth), bf16),
            dma((2, n_head)),
            dma((2, n_rail, n_head)),
            dma((2, n_head)),
            dma((2, n_rail)),
        ],
        compiler_params=pltpu.CompilerParams(
            collective_id=0, has_side_effects=True, vmem_limit_bytes=VMEM_LIMIT
        ),
        name="gather_rows",
    )(key_proj.reshape(share, kv_heads * depth), value_proj.reshape(share, kv_heads * depth))

    rows = TILE * group
    per_shard = row_count // TILE
    most = tiles // 4
    smem = pl.BlockSpec(memory_space=pltpu.SMEM)
    tile_spec = pl.BlockSpec((rows, depth), lambda t: (t, 0))
    attended, query_grad, partial = pl.pallas_call(
        functools.partial(attention_kernel, tiles, group, docs),
        grid=(per_shard,),
        out_shape=(
            jax.ShapeDtypeStruct((row_count * group, depth), bf16),
            jax.ShapeDtypeStruct((row_count * group, depth), bf16),
            jax.ShapeDtypeStruct((2, tiles, TILE, depth), bf16),
        ),
        in_specs=[smem, smem, tile_spec, tile_spec, vmem],
        out_specs=(tile_spec, tile_spec, vmem),
        scratch_shapes=[
            pltpu.SMEM((tiles,), jnp.int32),
            pltpu.VMEM((tiles, depth, TILE), bf16),
            pltpu.VMEM((tiles, depth, TILE), bf16),
            pltpu.VMEM((depth, rows), bf16),
            pltpu.VMEM((depth, rows), bf16),
            pltpu.VMEM((rows, depth), bf16),
            pltpu.VMEM((depth, rows), bf16),
            pltpu.VMEM((most, 2 * TILE, rows), f32),
            pltpu.VMEM((most, 2 * TILE, rows), bf16),
            pltpu.VMEM((depth, rows), f32),
            pltpu.VMEM((depth, rows), f32),
            pltpu.VMEM((2, tiles, TILE, depth), f32),
            pltpu.VMEM((TILE, rows), jnp.int32),
        ],
        compiler_params=pltpu.CompilerParams(vmem_limit_bytes=VMEM_LIMIT),
        name="attention_tiles",
    )(
        tile_order,
        doc_tiles,
        queries.reshape(row_count * group, depth),
        out_grad.reshape(row_count * group, depth),
        rows_kv.reshape(2, tiles, TILE, depth),
    )

    key_grad, value_grad = pl.pallas_call(
        functools.partial(reduce_kernel, n_ctx, n_head),
        out_shape=(
            jax.ShapeDtypeStruct((share, kv_heads * depth), bf16),
            jax.ShapeDtypeStruct((share, kv_heads * depth), bf16),
        ),
        in_specs=[vmem],
        out_specs=(vmem, vmem),
        scratch_shapes=[
            pltpu.VMEM((n_rail, 2, n_head, share, depth), bf16),
            pltpu.VMEM((n_rail, 2, n_head, share, depth), bf16),
            pltpu.VMEM((n_rail, 2, n_head, share, depth), bf16),
            pltpu.VMEM((n_head, 2, share, depth), bf16),
            pltpu.VMEM((n_head, 2, share, depth), bf16),
            dma((2, n_rail)),
            dma((2, n_rail)),
            dma((2, n_head)),
        ],
        compiler_params=pltpu.CompilerParams(
            collective_id=1, has_side_effects=True, vmem_limit_bytes=VMEM_LIMIT
        ),
        name="sum_gradients",
    )(partial.reshape(2, n_ctx, n_head, share, depth))

    return (
        attended.reshape(row_count, group, depth),
        query_grad.reshape(row_count, group, depth),
        key_grad.reshape(share, kv_heads, depth),
        value_grad.reshape(share, kv_heads, depth),
    )


def solution(mesh):
    in_specs = (
        P("ctx", "head", None),
        P(("ctx", "head"), None, None),
        P(("ctx", "head"), None, None),
        P("ctx", "head", None),
        P(),
        P(),
    )
    out_specs = (
        P("ctx", "head", None),
        P("ctx", "head", None),
        P(("ctx", "head"), None, None),
        P(("ctx", "head"), None, None),
    )
    return jax.shard_map(
        functools.partial(body, mesh.shape["ctx"], mesh.shape["head"]),
        mesh=mesh,
        in_specs=in_specs,
        out_specs=out_specs,
        check_vma=False,
    )
```

time: 185 us -> 56.9 us (0.31)
  Pallas kernels: 0 us -> 52.5 us
  waiting for transfers between devices: 43.8 us -> 0 us
  other arithmetic: 43.5 us -> 0 us
  matrix products: 38.5 us -> 0 us
  starting transfers between devices: 33.8 us -> 0 us
  local copies, waits for them, and re-layouts: 21 us -> 2.84 us
    pallas_call x0 -> x3, Pallas kernels: none -> 52.5 us  [the longest x1 25.8 us: body(): pl.pallas_call(functools.partial(reduce_kernel, n_ctx, n_head), out_shape...]
    dot_general x56 -> x0, matrix products: 38.5 us -> none  [the longest x16 13.9 us: block_scores(): jnp.einsum('tngd,knd->tngk', query_block, key_block, preferred_element_ty...]
    ppermute x46 -> x0, waiting for transfers between devices: 34.9 us -> none  [from_behind(): return lax.ppermute(value, axis, pairs)]
    ppermute x46 -> x0, starting transfers between devices: 18.8 us -> none  [from_behind(): return lax.ppermute(value, axis, pairs)]
    all_to_all x4 -> x0, starting transfers between devices: 15 us -> none  [the longest x1 5.16 us: body(): lax.all_to_all(key_proj, 'head', split_axis=1, concat_axis=0, tiled=True)]
    reduce_sum x25 -> x0, other arithmetic: 14.6 us -> none  [the longest x16 7.69 us: row_info(): jnp.sum((shard_tiles[:, None] >= doc_ends[None, :]).astype(jnp.int32), ax...]
    unnamed x39 -> x8, local copies, waits for them, and re-layouts: 10.8 us -> 0.65 us
    le x15 -> x0, other arithmetic: 9.68 us -> none  [block_mask(): key_pos[None, :] <= query_pos[:, None]]
  transfers between devices with their start and end apart: 50 -> 0, of which waited for: 27 -> 0; matrix products, arithmetic and copies ran while one was open for 43% -> 0% of each run, Pallas kernels for 0% -> 0%
where the time goes in v1:
time: 56.9 us; the launch traced here: 56.1 us
  Pallas kernels  52.5 us (92%)
  local copies, waits for them, and re-layouts  2.84 us (5%)
  between operations  0.7 us (1%)
    pallas_call x1, Pallas kernels, body(): pl.pallas_call(functools.partial(reduce_kernel, n_ctx, n_head), out_shape...  25.8 us
    pallas_call x1, Pallas kernels, body(): pl.pallas_call(functools.partial(gather_kernel, n_ctx, n_head), out_shape...  19.8 us
    pallas_call x1, Pallas kernels, body(): pl.pallas_call(functools.partial(attention_kernel, tiles, group, docs), g...  6.9 us

profile of v1, /device:TPU:0, one launch (start us, length us, event | category | flops | bytes accessed | tf_op | source)
XLA Modules:
  0.0 56.1 jit_solution(4061597111340541160)
XLA Ops:
  0.6 0.9 %copy_bitcast_fusion = (bf16[64,512]{1,0:T(8,128)(2,1)S(1)}, bf16[64,512]{1,0:T(8,128)(2,1)S(1)}) fusion(bf16[8,8,4,128]{3,2,1,0:T(4,128)(2,1)} %bitcast.16, bf16[8,8,4,128]{3,2,1,0:T(4,128)(2,1)} %bitcast.17), kind=kLoop, calls=%fused_computation | loop fusion | bytes 262144 | tf_op jit(solution)/shard_map/reshape | solution.py:307
  1.5 0.0 copy-start
  1.5 0.0 copy-start.1
  1.5 19.8 %gather_rows.1 = bf16[2,8,4,64,128]{4,3,2,1,0:T(8,128)(2,1)S(1)} custom-call(bf16[64,512]{1,0:T(8,128)(2,1)S(1)} %get-tuple-element.15.k_ref, bf16[64,512]{1,0:T(8,128)(2,1)S(1)} %get-tuple-element.14.v_ref), custom_call_target="tpu_custom_call" | custom-call | tf_op jit(solution)/shard_map/gather_rows/pallas_call | solution.py:291
  21.4 0.0 copy-start.2
  21.4 0.0 copy-start.3
  21.4 0.0 copy-done
  21.4 0.0 copy-done.1
  21.4 0.6 %copy-done.2 = s32[16]{0:T(128)S(1)} copy-done((s32[16]{0:T(128)S(1)}, s32[16]{0:T(128)}, u32[]{:S(2)}) %copy-start.2) | copy-done | bytes 88
  22.0 0.0 copy-done.3
  22.0 6.9 %attention_tiles.1 = (bf16[2048,128]{1,0:T(8,128)(2,1)}, bf16[2048,128]{1,0:T(8,128)(2,1)}, bf16[2,16,128,128]{3,2,1,0:T(8,128)(2,1)S(1)}) custom-call(s32[16]{0:T(128)S(1)} %copy-done.2, s32[4]{0:T(128)S(1)} %copy-done.3, bf16[2048,128]{1,0:T(8,128)(2,1)S(1)} %bitcast.14, bf16[2048,128]{1,0:T(8,128)(2,1)S(1)} %bitcast.15, bf16[2,16,128,128]{3,2,1,0:T(8,128)(2,1)S(1)} %bitcast.12), custom_call_target="tpu_custom_call" | custom-call | tf_op jit(solution)/shard_map/attention_tiles/pallas_call | solution.py:314
  28.9 25.8 %sum_gradients.1 = (bf16[64,512]{1,0:T(8,128)(2,1)S(1)}, bf16[64,512]{1,0:T(8,128)(2,1)S(1)}) custom-call(bf16[2,8,4,64,128]{4,3,2,1,0:T(8,128)(2,1)S(1)} %bitcast.13), custom_call_target="tpu_custom_call" | custom-call | tf_op jit(solution)/shard_map/sum_gradients/pallas_call | solution.py:349
  54.8 0.6 %reshape.46 = bf16[64,4,128]{2,1,0:T(4,128)(2,1)} reshape(bf16[64,512]{1,0:T(8,128)(2,1)S(1)} %get-tuple-element.12) | data formatting | bytes 131072 | tf_op jit(solution)/shard_map/reshape | solution.py:376
  55.4 0.6 %reshape.47 = bf16[64,4,128]{2,1,0:T(4,128)(2,1)} reshape(bf16[64,512]{1,0:T(8,128)(2,1)S(1)} %get-tuple-element.13) | data formatting | bytes 131072 | tf_op jit(solution)/shard_map/reshape | solution.py:377
Async XLA Ops:
  1.5 19.9 %copy-start = (bf16[256,8,128]{2,1,0:T(8,128)(2,1)S(1)}, bf16[256,8,128]{2,1,0:T(8,128)(2,1)}, u32[]{:S(2)}) copy-start(bf16[256,8,128]{2,1,0:T(8,128)(2,1)} %param.6) | copy-start | bytes 1572868
  1.5 19.9 %copy-start.1 = (bf16[256,8,128]{2,1,0:T(8,128)(2,1)S(1)}, bf16[256,8,128]{2,1,0:T(8,128)(2,1)}, u32[]{:S(2)}) copy-start(bf16[256,8,128]{2,1,0:T(8,128)(2,1)} %param.9) | copy-start | bytes 1572868
  21.4 0.7 %copy-start.2 = (s32[16]{0:T(128)S(1)}, s32[16]{0:T(128)}, u32[]{:S(2)}) copy-start(s32[16]{0:T(128)} %order_ref.1) | copy-start | bytes 196
  21.4 0.7 %copy-start.3 = (s32[4]{0:T(128)S(1)}, s32[4]{0:T(128)}, u32[]{:S(2)}) copy-start(s32[4]{0:T(128)} %docs_ref.1) | copy-start | bytes 52

commit v2 on v1

--- a/solution.py
+++ b/solution.py
@@ -52,7 +52,9 @@
     )
 
 
-def gather_kernel(n_ctx, n_head, k_ref, v_ref, out_ref, turned, head_sems, rail_sems, sib_sems, fwd_sems):
+def gather_kernel(
+    n_ctx, n_head, k_ref, v_ref, out_ref, turned, head_sems, right_sems, left_sems, sib_sems
+):
     ctx, head, core, rail, n_rail, sibling = peers(n_ctx, n_head)
     for g in range(n_head):
         turned[g, 0] = k_ref[:, g * 128 : (g + 1) * 128]
@@ -69,108 +71,192 @@
     for d in range(1, n_head):
         head_copy(d).start()
 
-    def rail_copy(dz, d):
-        source = lax.rem(head + n_head - d, n_head)
-        target = lax.rem(rail + dz, n_rail) * 2 + core
-        block = out_ref.at[:, ctx, source]
-        return remote(block, block, rail_sems.at[0, dz, d], rail_sems.at[1, dz, d], target, head)
-
-    def sib_copy(d):
-        source = lax.rem(head + n_head - d, n_head)
-        block = out_ref.at[:, ctx, source]
-        return remote(block, block, sib_sems.at[0, d], sib_sems.at[1, d], sibling, head)
-
-    def fwd_copy(dz):
-        block = out_ref.at[:, lax.rem(rail + n_rail - dz, n_rail) * 2 + core]
-        return remote(block, block, fwd_sems.at[0, dz], fwd_sems.at[1, dz], sibling, head)
+    def block_of(source, d):
+        return out_ref.at[:, source * 2 + core, lax.rem(head + n_head - d, n_head)]
+
+    def line_copy(way, hops, d):
+        sems = right_sems if way > 0 else left_sems
+        block = block_of(jnp.clip(rail - way * hops, 0, n_rail - 1), d)
+        target = jnp.clip(rail + way, 0, n_rail - 1) * 2 + core
+        return remote(block, block, sems.at[0, hops, d], sems.at[1, hops, d], target, head)
+
+    def line_recv(way, hops, d):
+        sems = right_sems if way > 0 else left_sems
+        block = block_of(jnp.clip(rail - way * hops, 0, n_rail - 1), d)
+        source = jnp.clip(rail - way, 0, n_rail - 1) * 2 + core
+        return remote(block, block, sems.at[0, hops - 1, d], sems.at[1, hops - 1, d], source, head)
+
+    def sib_copy(source, d):
+        block = block_of(source, d)
+        return remote(block, block, sib_sems.at[0, source, d], sib_sems.at[1, source, d], sibling, head)
+
+    def room(way):
+        return n_rail - 1 - rail if way > 0 else rail
 
     for d in range(n_head):
         if d > 0:
             head_copy(d).wait_recv()
-        for dz in range(1, n_rail):
-            rail_copy(dz, d).start()
-        sib_copy(d).start()
-    for dz in range(1, n_rail):
+        for way in (1, -1):
+            @pl.when(room(way) > 0)
+            def _():
+                line_copy(way, 0, d).start()
+        sib_copy(rail, d).start()
+    for hops in range(1, n_rail):
         for d in range(n_head):
-            rail_copy(dz, d).wait_recv()
-        fwd_copy(dz).start()
+            for way in (1, -1):
+                @pl.when(room(-way) >= hops)
+                def _():
+                    line_recv(way, hops, d).wait_recv()
+
+                    @pl.when(room(way) > 0)
+                    def _():
+                        line_copy(way, hops, d).start()
+                    sib_copy(rail - way * hops, d).start()
     for d in range(1, n_head):
         head_copy(d).wait_send()
     for d in range(n_head):
-        for dz in range(1, n_rail):
-            rail_copy(dz, d).wait_send()
-        sib_copy(d).wait()
-    for dz in range(1, n_rail):
-        fwd_copy(dz).wait()
+        for hops in range(n_rail - 1):
+            for way in (1, -1):
+                @pl.when((room(way) > 0) & (room(-way) >= hops))
+                def _():
+                    line_copy(way, hops, d).wait_send()
+        for source in range(n_rail):
+            sib_copy(source, d).wait_send()
+            block = out_ref.at[:, source * 2 + 1 - core, lax.rem(head + n_head - d, n_head)]
+            remote(
+                block, block, sib_sems.at[0, source, d], sib_sems.at[1, source, d], sibling, head
+            ).wait_recv()
 
 
 def reduce_kernel(
-    n_ctx, n_head, part_ref, k_ref, v_ref, sib_in, summed, rail_in, turned, head_in,
-    sib_sems, rail_sems, head_sems,
+    n_ctx, n_head, part_ref, k_ref, v_ref, sib_in, right_out, left_out, right_in, left_in,
+    turned, head_in, sib_sems, right_sems, left_sems, head_sems,
 ):
     ctx, head, core, rail, n_rail, sibling = peers(n_ctx, n_head)
+    scale = 1.0 / math.sqrt(128)
     entry_barrier(ctx, head, core, rail, n_rail, sibling, n_head)
 
-    def rail_of(dz):
-        return lax.rem(rail + dz, n_rail)
-
-    def sib_copy(dz):
+    def sib_copy(dest):
         return remote(
-            part_ref.at[:, rail_of(dz) * 2 + (1 - core)],
-            sib_in.at[dz],
-            sib_sems.at[0, dz],
-            sib_sems.at[1, dz],
+            part_ref.at[:, dest * 2 + (1 - core)],
+            sib_in.at[dest],
+            sib_sems.at[0, dest],
+            sib_sems.at[1, dest],
             sibling,
             head,
         )
 
-    def rail_copy(dz):
+    def line_copy(way, dest, g):
+        sems, out, into = (
+            (right_sems, right_out, right_in) if way > 0 else (left_sems, left_out, left_in)
+        )
+        target = jnp.clip(rail + way, 0, n_rail - 1) * 2 + core
         return remote(
-            summed.at[dz], rail_in.at[dz], rail_sems.at[0, dz], rail_sems.at[1, dz],
-            rail_of(dz) * 2 + core, head,
-        )
-
-    def head_copy(d):
-        target = lax.rem(head + d, n_head)
+            out.at[dest, g], into.at[dest, g], sems.at[0, dest, g], sems.at[1, dest, g], target, head
+        )
+
+    def head_copy(g, place):
         return remote(
-            turned.at[target], head_in.at[d], head_sems.at[0, d], head_sems.at[1, d], ctx, target
-        )
-
-    order = list(range(n_rail - 1, 0, -1)) + [0]
-    for dz in order:
-        sib_copy(dz).start()
-    total = None
-    for dz in order:
-        sib_copy(dz).wait_recv()
-        own = part_ref[:, rail_of(dz) * 2 + core].astype(jnp.float32)
-        both = own + sib_in[dz].astype(jnp.float32)
-        if dz > 0:
-            summed[dz] = both.astype(jnp.bfloat16)
-            rail_copy(dz).start()
-        else:
-            total = both
-    for dz in range(1, n_rail):
-        rail_copy(dz).wait_recv()
-        total = total + rail_in[dz].astype(jnp.float32)
-    scale = 1.0 / math.sqrt(128)
+            turned.at[g], head_in.at[place], head_sems.at[0, g], head_sems.at[1, place], ctx, g
+        )
+
+    def pair_sum(dest, g):
+        own = part_ref[:, dest * 2 + core, g].astype(jnp.float32)
+        return own + sib_in[dest, :, g].astype(jnp.float32)
+
+    order = []
+    for i in range(n_rail):
+        for dest in (n_rail - 1 - i, i):
+            if dest not in order:
+                order.append(dest)
+    for dest in order:
+        sib_copy(dest).start()
+
+    def send_on(way, dest):
+        out, into = (right_out, right_in) if way > 0 else (left_out, left_in)
+        first = rail == (0 if way > 0 else n_rail - 1)
+
+        @pl.loop(0, n_head)
+        def _(g):
+            @pl.when(first)
+            def _():
+                out[dest, g] = pair_sum(dest, g).astype(jnp.bfloat16)
+
+            @pl.when(jnp.logical_not(first))
+            def _():
+                line_copy(way, dest, g).wait_recv()
+                both = pair_sum(dest, g) + into[dest, g].astype(jnp.float32)
+                out[dest, g] = both.astype(jnp.bfloat16)
+            line_copy(way, dest, g).start()
+
+    arrived = set()
+    for i in range(n_rail):
+        for way, dest in ((1, n_rail - 1 - i), (-1, i)):
+            if dest not in arrived:
+                arrived.add(dest)
+                sib_copy(dest).wait_recv()
+            if way > 0 and dest > 0:
+                @pl.when(dest > rail)
+                def _():
+                    send_on(1, dest)
+            if way < 0 and dest < n_rail - 1:
+                @pl.when(dest < rail)
+                def _():
+                    send_on(-1, dest)
+
+    @pl.loop(0, n_head)
+    def _(g):
+        @pl.when(rail > 0)
+        def _():
+            line_copy(1, rail, g).wait_recv()
+
+        @pl.when(rail < n_rail - 1)
+        def _():
+            line_copy(-1, rail, g).wait_recv()
+        def finish(total):
+            turned[g, 0] = (total[0] * scale).astype(jnp.bfloat16)
+            turned[g, 1] = total[1].astype(jnp.bfloat16)
+
+        @pl.when(rail == 0)
+        def _():
+            finish(pair_sum(rail, g) + left_in[rail, g].astype(jnp.float32))
+
+        @pl.when(rail == n_rail - 1)
+        def _():
+            finish(pair_sum(rail, g) + right_in[rail, g].astype(jnp.float32))
+
+        @pl.when((rail > 0) & (rail < n_rail - 1))
+        def _():
+            sides = right_in[rail, g].astype(jnp.float32) + left_in[rail, g].astype(jnp.float32)
+            finish(pair_sum(rail, g) + sides)
+
+        @pl.when(g != head)
+        def _():
+            head_copy(g, head).start()
+
+    head_in[head] = turned[head]
     for g in range(n_head):
-        turned[g, 0] = (total[0, g] * scale).astype(jnp.bfloat16)
-        turned[g, 1] = total[1, g].astype(jnp.bfloat16)
-    for d in range(1, n_head):
-        head_copy(d).start()
-    head_in[0] = turned[head]
-    for d in range(1, n_head):
-        head_copy(d).wait_recv()
+        @pl.when(g != head)
+        def _():
+            head_copy(g, g).wait_recv()
+        k_ref[:, g * 128 : (g + 1) * 128] = head_in[g, 0]
+        v_ref[:, g * 128 : (g + 1) * 128] = head_in[g, 1]
     for g in range(n_head):
-        place = lax.rem(head - g + n_head, n_head)
-        k_ref[:, g * 128 : (g + 1) * 128] = head_in[place, 0]
-        v_ref[:, g * 128 : (g + 1) * 128] = head_in[place, 1]
-    for dz in range(n_rail):
-        sib_copy(dz).wait_send()
-    for dz in range(1, n_rail):
-        rail_copy(dz).wait_send()
-    for d in range(1, n_head):
-        head_copy(d).wait_send()
+        @pl.when(g != head)
+        def _():
+            head_copy(g, head).wait_send()
+    for dest in range(n_rail):
+        sib_copy(dest).wait_send()
+
+        @pl.loop(0, n_head)
+        def _(g):
+            @pl.when(dest > rail)
+            def _():
+                line_copy(1, dest, g).wait_send()
+
+            @pl.when(dest < rail)
+            def _():
+                line_copy(-1, dest, g).wait_send()
 
 
 def dot(a, b):
@@ -297,8 +383,8 @@
             pltpu.VMEM((n_head, 2, share, depth), bf16),
             dma((2, n_head)),
             dma((2, n_rail, n_head)),
-            dma((2, n_head)),
-            dma((2, n_rail)),
+            dma((2, n_rail, n_head)),
+            dma((2, n_rail, n_head)),
         ],
         compiler_params=pltpu.CompilerParams(
             collective_id=0, has_side_effects=True, vmem_limit_bytes=VMEM_LIMIT
@@ -356,12 +442,15 @@
         out_specs=(vmem, vmem),
         scratch_shapes=[
             pltpu.VMEM((n_rail, 2, n_head, share, depth), bf16),
-            pltpu.VMEM((n_rail, 2, n_head, share, depth), bf16),
-            pltpu.VMEM((n_rail, 2, n_head, share, depth), bf16),
+            pltpu.VMEM((n_rail, n_head, 2, share, depth), bf16),
+            pltpu.VMEM((n_rail, n_head, 2, share, depth), bf16),
+            pltpu.VMEM((n_rail, n_head, 2, share, depth), bf16),
+            pltpu.VMEM((n_rail, n_head, 2, share, depth), bf16),
             pltpu.VMEM((n_head, 2, share, depth), bf16),
             pltpu.VMEM((n_head, 2, share, depth), bf16),
             dma((2, n_rail)),
-            dma((2, n_rail)),
+            dma((2, n_rail, n_head)),
+            dma((2, n_rail, n_head)),
             dma((2, n_head)),
         ],
         compiler_params=pltpu.CompilerParams(

time: 56.9 us -> 56.5 us (level); the launches traced: 56.1 us -> 56.6 us
    pallas_call x1, Pallas kernels: 25.8 us -> 23.8 us  [body(): pl.pallas_call(functools.partial(reduce_kernel, n_ctx, n_head), out_shape...]
    pallas_call x1, Pallas kernels: 6.9 us -> 8.37 us  [body(): pl.pallas_call(functools.partial(attention_kernel, tiles, group, docs), g...]
    pallas_call x1, Pallas kernels: 19.8 us -> 20.9 us  [body(): pl.pallas_call(functools.partial(gather_kernel, n_ctx, n_head), out_shape...]
where the time goes in v2:
time: 56.5 us; the launch traced here: 56.6 us
  Pallas kernels  53 us (94%)
  local copies, waits for them, and re-layouts  2.84 us (5%)
  between operations  0.7 us (1%)
    pallas_call x1, Pallas kernels, body(): pl.pallas_call(functools.partial(reduce_kernel, n_ctx, n_head), out_shape...  23.8 us
    pallas_call x1, Pallas kernels, body(): pl.pallas_call(functools.partial(gather_kernel, n_ctx, n_head), out_shape...  20.9 us
    pallas_call x1, Pallas kernels, body(): pl.pallas_call(functools.partial(attention_kernel, tiles, group, docs), g...  8.37 us

profile of v2, /device:TPU:0, one launch (start us, length us, event | category | flops | bytes accessed | tf_op | source)
XLA Modules:
  0.0 56.6 jit_solution(17148164290345199760)
XLA Ops:
  0.6 0.9 %copy_bitcast_fusion = (bf16[64,512]{1,0:T(8,128)(2,1)S(1)}, bf16[64,512]{1,0:T(8,128)(2,1)S(1)}) fusion(bf16[8,8,4,128]{3,2,1,0:T(4,128)(2,1)} %bitcast.16, bf16[8,8,4,128]{3,2,1,0:T(4,128)(2,1)} %bitcast.17), kind=kLoop, calls=%fused_computation | loop fusion | bytes 262144 | tf_op jit(solution)/shard_map/reshape | solution.py:393
  1.5 0.0 copy-start
  1.5 0.0 copy-start.1
  1.5 20.9 %gather_rows.1 = bf16[2,8,4,64,128]{4,3,2,1,0:T(8,128)(2,1)S(1)} custom-call(bf16[64,512]{1,0:T(8,128)(2,1)S(1)} %get-tuple-element.15.k_ref, bf16[64,512]{1,0:T(8,128)(2,1)S(1)} %get-tuple-element.14.v_ref), custom_call_target="tpu_custom_call" | custom-call | tf_op jit(solution)/shard_map/gather_rows/pallas_call | solution.py:377
  22.4 0.0 copy-start.2
  22.5 0.0 copy-start.3
  22.5 0.0 copy-done
  22.5 0.0 copy-done.1
  22.5 0.6 %copy-done.2 = s32[16]{0:T(128)S(1)} copy-done((s32[16]{0:T(128)S(1)}, s32[16]{0:T(128)}, u32[]{:S(2)}) %copy-start.2) | copy-done | bytes 88
  23.1 0.0 copy-done.3
  23.1 8.4 %attention_tiles.1 = (bf16[2048,128]{1,0:T(8,128)(2,1)}, bf16[2048,128]{1,0:T(8,128)(2,1)}, bf16[2,16,128,128]{3,2,1,0:T(8,128)(2,1)S(1)}) custom-call(s32[16]{0:T(128)S(1)} %copy-done.2, s32[4]{0:T(128)S(1)} %copy-done.3, bf16[2048,128]{1,0:T(8,128)(2,1)S(1)} %bitcast.14, bf16[2048,128]{1,0:T(8,128)(2,1)S(1)} %bitcast.15, bf16[2,16,128,128]{3,2,1,0:T(8,128)(2,1)S(1)} %bitcast.12), custom_call_target="tpu_custom_call" | custom-call | tf_op jit(solution)/shard_map/attention_tiles/pallas_call | solution.py:400
  31.5 23.8 %sum_gradients.1 = (bf16[64,512]{1,0:T(8,128)(2,1)S(1)}, bf16[64,512]{1,0:T(8,128)(2,1)S(1)}) custom-call(bf16[2,8,4,64,128]{4,3,2,1,0:T(8,128)(2,1)S(1)} %bitcast.13), custom_call_target="tpu_custom_call" | custom-call | tf_op jit(solution)/shard_map/sum_gradients/pallas_call | solution.py:435
  55.3 0.6 %reshape.46 = bf16[64,4,128]{2,1,0:T(4,128)(2,1)} reshape(bf16[64,512]{1,0:T(8,128)(2,1)S(1)} %get-tuple-element.12) | data formatting | bytes 131072 | tf_op jit(solution)/shard_map/reshape | solution.py:465
  55.9 0.6 %reshape.47 = bf16[64,4,128]{2,1,0:T(4,128)(2,1)} reshape(bf16[64,512]{1,0:T(8,128)(2,1)S(1)} %get-tuple-element.13) | data formatting | bytes 131072 | tf_op jit(solution)/shard_map/reshape | solution.py:466
Async XLA Ops:
  1.5 20.9 %copy-start = (bf16[256,8,128]{2,1,0:T(8,128)(2,1)S(1)}, bf16[256,8,128]{2,1,0:T(8,128)(2,1)}, u32[]{:S(2)}) copy-start(bf16[256,8,128]{2,1,0:T(8,128)(2,1)} %param.6) | copy-start | bytes 1572868
  1.5 20.9 %copy-start.1 = (bf16[256,8,128]{2,1,0:T(8,128)(2,1)S(1)}, bf16[256,8,128]{2,1,0:T(8,128)(2,1)}, u32[]{:S(2)}) copy-start(bf16[256,8,128]{2,1,0:T(8,128)(2,1)} %param.9) | copy-start | bytes 1572868
  22.4 0.7 %copy-start.2 = (s32[16]{0:T(128)S(1)}, s32[16]{0:T(128)}, u32[]{:S(2)}) copy-start(s32[16]{0:T(128)} %order_ref.1) | copy-start | bytes 196
  22.5 0.7 %copy-start.3 = (s32[4]{0:T(128)S(1)}, s32[4]{0:T(128)}, u32[]{:S(2)}) copy-start(s32[4]{0:T(128)} %docs_ref.1) | copy-start | bytes 52

commit v3 on v0

v3 whole, which is shorter than its diff:
```python
import functools
import math

import jax
import jax.numpy as jnp
from jax import lax
from jax.experimental import pallas as pl
from jax.experimental.pallas import tpu as pltpu
from jax.sharding import PartitionSpec as P

TILE = 128
NEG = -1e30
MESH = pl.DeviceIdType.MESH
VMEM_LIMIT = 48 * 1024 * 1024


def peers(n_ctx, n_head):
    ctx = lax.axis_index("ctx")
    head = lax.axis_index("head")
    core = lax.rem(ctx, 2)
    rail = lax.div(ctx, 2)
    n_rail = n_ctx // 2
    sibling = rail * 2 + (1 - core)
    return ctx, head, core, rail, n_rail, sibling


def entry_barrier(ctx, head, core, rail, n_rail, sibling, n_head):
    barrier = pltpu.get_barrier_semaphore()
    for d in range(1, n_head):
        pl.semaphore_signal(
            barrier, inc=1, device_id=(ctx, lax.rem(head + d, n_head)), device_id_type=MESH
        )
    for d in range(1, n_rail):
        pl.semaphore_signal(
            barrier,
            inc=1,
            device_id=(lax.rem(rail + d, n_rail) * 2 + core, head),
            device_id_type=MESH,
        )
    pl.semaphore_signal(barrier, inc=1, device_id=(sibling, head), device_id_type=MESH)
    pl.semaphore_wait(barrier, n_head - 1 + n_rail - 1 + 1)


def remote(src, dst, send, recv, ctx, head):
    return pltpu.make_async_remote_copy(
        src_ref=src,
        dst_ref=dst,
        send_sem=send,
        recv_sem=recv,
        device_id=(ctx, head),
        device_id_type=MESH,
    )


def dot(a, b):
    return jnp.dot(a, b, preferred_element_type=jnp.float32)


def fused_kernel(
    n_ctx, n_head, tiles, group, docs, per_shard, share,
    order_ref, docs_ref, q_ref, g_ref, k_ref, v_ref,
    o_ref, dq_ref, kg_ref, vg_ref,
    slots, turned, k_buf, v_buf, kw, kw_t, vw, vw_t, q_t, g_t, g_s, weights, dscores, o_t,
    inverse, delta, dkw, dvw, part_k, part_v, sib_k, sib_v, out_k, out_v, in_k, in_v,
    back, head_in,
    head_sems, rail_sems, sib_sems, fwd_sems, psib_sems, prail_sems, phead_sems,
):
    f32, bf16 = jnp.float32, jnp.bfloat16
    ctx, head, core, rail, n_rail, sibling = peers(n_ctx, n_head)
    parts = TILE // share
    window = tiles // 2
    total_chunks, chunk, depth = q_ref.shape
    chunks = total_chunks // per_shard
    scale = 1.0 / math.sqrt(depth)
    bufs = (k_buf, v_buf)

    def rows_of(buf, c, h):
        return buf.at[c * per_shard + lax.div(h, parts), lax.rem(h, parts)]

    def rail_at(dz):
        return lax.rem(rail + dz, n_rail) * 2 + core

    for x, source in enumerate((k_ref, v_ref)):
        for g in range(n_head):
            turned[x, g] = source[:, g * depth : (g + 1) * depth]
    for x in range(2):
        bufs[x][ctx * per_shard + lax.div(head, parts), lax.rem(head, parts)] = turned[x, head]
    entry_barrier(ctx, head, core, rail, n_rail, sibling, n_head)

    def head_copy(x, d):
        target = lax.rem(head + d, n_head)
        return remote(
            turned.at[x, target], rows_of(bufs[x], ctx, head), head_sems.at[x, 0, d],
            head_sems.at[x, 1, d], ctx, target,
        )

    def rail_copy(x, dz, d):
        rows = rows_of(bufs[x], ctx, lax.rem(head + n_head - d, n_head))
        return remote(
            rows, rows, rail_sems.at[x, 0, dz, d], rail_sems.at[x, 1, dz, d], rail_at(dz), head
        )

    def sib_copy(x, d):
        rows = rows_of(bufs[x], ctx, lax.rem(head + n_head - d, n_head))
        return remote(rows, rows, sib_sems.at[x, 0, d], sib_sems.at[x, 1, d], sibling, head)

    def fwd_copy(x, dz):
        source = lax.rem(rail + n_rail - dz, n_rail) * 2 + core
        rows = bufs[x].at[pl.ds(source * per_shard, per_shard)]
        return remote(rows, rows, fwd_sems.at[x, 0, dz], fwd_sems.at[x, 1, dz], sibling, head)

    def hand_on(x):
        for dz in range(1, n_rail):
            for d in range(n_head):
                rail_copy(x, dz, d).wait_recv()
            fwd_copy(x, dz).start()

    def arrive(x):
        for d in range(n_head):
            sib_copy(x, d).wait_recv()
        for dz in range(1, n_rail):
            fwd_copy(x, dz).wait_recv()

    for x in range(2):
        for d in range(1, n_head):
            head_copy(x, d).start()
    for x in range(2):
        for d in range(n_head):
            if d > 0:
                head_copy(x, d).wait_recv()
            for dz in range(n_rail - 1, 0, -1):
                rail_copy(x, dz, d).start()
            sib_copy(x, d).start()

    mine, count = [], []
    for t in range(per_shard):
        tile = order_ref[ctx * per_shard + t]
        end, first = 0, 0
        for d in range(docs):
            end = end + docs_ref[d]
            first = jnp.where(end <= tile, end, first)
        mine.append(tile)
        count.append(tile - first + 1)
        for w in range(window):
            wanted = jnp.maximum(tile - w, 0)
            slot = 0
            for s in range(tiles):
                slot = jnp.where(order_ref[s] == wanted, s, slot)
            slots[t * window + w] = slot
        dkw[t, window] = jnp.zeros((TILE, depth), f32)
        dvw[t, window] = jnp.zeros((TILE, depth), f32)

    @pl.loop(0, total_chunks)
    def _(n):
        q_t[n] = q_ref[n].T
        g_t[n] = g_ref[n].T

    def fill(into, turned_into, buf):
        for t in range(per_shard):
            @pl.loop(0, window)
            def _(w):
                block = buf[slots[t * window + w]].reshape(TILE, depth)
                into[t, w] = block
                turned_into[t, w] = block.T

    hand_on(0)
    arrive(0)
    fill(kw, kw_t, k_buf)

    for t in range(per_shard):
        @pl.loop(t * chunks, (t + 1) * chunks)
        def _(n):
            s = dot(kw[t].reshape(window * TILE, depth), q_t[n])
            key = lax.broadcasted_iota(jnp.int32, (TILE, chunk), 0)
            row = lax.div(lax.broadcasted_iota(jnp.int32, (TILE, chunk), 1), group)
            seen = key - row <= (n - t * chunks) * (chunk // group)
            pieces = [jnp.where(seen, s[:TILE], NEG)]
            for w in range(1, window):
                pieces.append(s[w * TILE : (w + 1) * TILE] + jnp.where(w < count[t], 0.0, NEG))
            top = pieces[0]
            for piece in pieces[1:]:
                top = jnp.maximum(top, piece)
            top = jnp.max(top, axis=0, keepdims=True)
            total = jnp.zeros((TILE, chunk), f32)
            for w, piece in enumerate(pieces):
                e = jnp.exp2((piece - top) * (scale * math.log2(math.e)))
                total = total + e
                weights[n, w * TILE : (w + 1) * TILE] = e.astype(bf16)
            inverse[n] = 1.0 / jnp.sum(total, axis=0, keepdims=True)

    hand_on(1)
    arrive(1)
    fill(vw, vw_t, v_buf)

    def side(ref, t):
        return jnp.concatenate([ref[t, w] for w in range(window)], axis=1)

    for t in range(per_shard):
        @pl.loop(t * chunks, (t + 1) * chunks)
        def _(n):
            out = (dot(side(vw_t, t), weights[n]) * inverse[n]).astype(bf16)
            o_t[n] = out
            grads = g_t[n].astype(f32)
            delta[n] = jnp.sum(grads * out.astype(f32), axis=0, keepdims=True) * inverse[n]
            scaled = (grads * inverse[n]).astype(bf16)
            g_t[n] = scaled
            g_s[n] = scaled.T

    def by_key(into, left, right):
        for t in range(per_shard):
            total = dot(left[t * chunks], right[t * chunks])
            for c in range(1, chunks):
                total = total + dot(left[t * chunks + c], right[t * chunks + c])
            into[t, 0:window] = total.reshape(window, TILE, depth)

    def by_slot(part, by_window):
        @pl.loop(0, tiles)
        def _(s):
            total = None
            for t in range(per_shard):
                w = mine[t] - order_ref[s]
                term = by_window[t, jnp.where((w >= 0) & (w < count[t]), w, window)]
                total = term if total is None else total + term
            part[s] = total.astype(bf16).reshape(parts, share, depth)

    part = (part_k, part_v)
    sib_in = (sib_k, sib_v)
    outs = (out_k, out_v)
    ins = (in_k, in_v)

    def psib_copy(x, dz):
        rows = part[x].at[pl.ds((lax.rem(rail + dz, n_rail) * 2 + 1 - core) * per_shard, per_shard)]
        return remote(
            rows, sib_in[x].at[dz], psib_sems.at[x, 0, dz], psib_sems.at[x, 1, dz], sibling, head
        )

    def prail_copy(x, dz):
        return remote(
            outs[x].at[dz], ins[x].at[dz], prail_sems.at[x, 0, dz], prail_sems.at[x, 1, dz],
            rail_at(dz), head,
        )

    def phead_copy(x, d):
        target = lax.rem(head + d, n_head)
        return remote(
            back.at[x, target], head_in.at[x, d], phead_sems.at[x, 0, d], phead_sems.at[x, 1, d],
            ctx, target,
        )

    far_first = list(range(n_rail - 1, -1, -1))

    def to_sibling(x):
        for dz in far_first:
            psib_copy(x, dz).start()

    def pair_sum(x, dz):
        own = part[x][pl.ds(rail_at(dz) * per_shard, per_shard)].astype(f32)
        return own + sib_in[x][dz].astype(f32)

    def to_rail(x):
        for dz in far_first[:-1]:
            psib_copy(x, dz).wait_recv()
            outs[x][dz] = pair_sum(x, dz).astype(bf16)
            prail_copy(x, dz).start()

    def to_heads(x, factor):
        psib_copy(x, 0).wait_recv()
        total = pair_sum(x, 0)
        for dz in range(1, n_rail):
            prail_copy(x, dz).wait_recv()
            total = total + ins[x][dz].astype(f32)
        if factor is not None:
            total = total * factor
        total = total.astype(bf16)
        for g in range(n_head):
            back[x, g] = total[g // parts, g % parts]
        for d in range(1, n_head):
            phead_copy(x, d).start()
        head_in[x, 0] = back[x, head]

    by_key(dvw, weights, g_s)
    by_slot(part_v, dvw)
    to_sibling(1)
    for t in range(per_shard):
        @pl.loop(t * chunks, (t + 1) * chunks)
        def _(n):
            dp = dot(vw[t].reshape(window * TILE, depth), g_t[n])
            dscores[n] = (weights[n].astype(f32) * (dp - delta[n])).astype(bf16)
    to_rail(1)
    by_key(dkw, dscores, q_ref)
    by_slot(part_k, dkw)
    to_sibling(0)

    @pl.loop(0, total_chunks)
    def _(n):
        o_ref[n] = o_t[n].T
    to_rail(0)
    for t in range(per_shard):
        @pl.loop(t * chunks, (t + 1) * chunks)
        def _(n):
            dq_ref[n] = (dot(side(kw_t, t), dscores[n]) * scale).astype(bf16).T
    to_heads(1, None)
    to_heads(0, scale)
    for x, result in ((1, vg_ref), (0, kg_ref)):
        for d in range(1, n_head):
            phead_copy(x, d).wait_recv()
        for g in range(n_head):
            place = lax.rem(head - g + n_head, n_head)
            result[:, g * depth : (g + 1) * depth] = head_in[x, place]

    for x in range(2):
        for d in range(n_head):
            if d > 0:
                head_copy(x, d).wait_send()
                phead_copy(x, d).wait_send()
            for dz in range(1, n_rail):
                rail_copy(x, dz, d).wait_send()
            sib_copy(x, d).wait_send()
        for dz in range(n_rail):
            psib_copy(x, dz).wait_send()
            if dz > 0:
                fwd_copy(x, dz).wait_send()
                prail_copy(x, dz).wait_send()


def body(n_ctx, n_head, queries, key_proj, value_proj, out_grad, tile_order, doc_tiles):
    row_count, group, depth = queries.shape
    share, kv_heads, _ = key_proj.shape
    tiles = tile_order.shape[0]
    docs = doc_tiles.shape[0]
    n_rail = n_ctx // 2
    per_shard = row_count // TILE
    parts = TILE // share
    window = tiles // 2
    chunk = 256
    nch = row_count * group // chunk
    bf16, f32 = jnp.bfloat16, jnp.float32
    vmem = pl.BlockSpec(memory_space=pltpu.VMEM)
    smem = pl.BlockSpec(memory_space=pltpu.SMEM)
    dma = pltpu.SemaphoreType.DMA
    wide = jax.ShapeDtypeStruct((nch, chunk, depth), bf16)
    thin = jax.ShapeDtypeStruct((share, kv_heads * depth), bf16)
    shard = (per_shard, parts, share, depth)
    attended, query_grad, key_grad, value_grad = pl.pallas_call(
        functools.partial(fused_kernel, n_ctx, n_head, tiles, group, docs, per_shard, share),
        out_shape=(wide, wide, thin, thin),
        in_specs=[smem, smem, vmem, vmem, vmem, vmem],
        out_specs=(vmem, vmem, vmem, vmem),
        scratch_shapes=[
            pltpu.SMEM((per_shard * window,), jnp.int32),
            pltpu.VMEM((2, n_head, share, depth), bf16),
            pltpu.VMEM((tiles, parts, share, depth), bf16),
            pltpu.VMEM((tiles, parts, share, depth), bf16),
            pltpu.VMEM((per_shard, window, TILE, depth), bf16),
            pltpu.VMEM((per_shard, window, depth, TILE), bf16),
            pltpu.VMEM((per_shard, window, TILE, depth), bf16),
            pltpu.VMEM((per_shard, window, depth, TILE), bf16),
            pltpu.VMEM((nch, depth, chunk), bf16),
            pltpu.VMEM((nch, depth, chunk), bf16),
            pltpu.VMEM((nch, chunk, depth), bf16),
            pltpu.VMEM((nch, window * TILE, chunk), bf16),
            pltpu.VMEM((nch, window * TILE, chunk), bf16),
            pltpu.VMEM((nch, depth, chunk), bf16),
            pltpu.VMEM((nch, 1, chunk), f32),
            pltpu.VMEM((nch, 1, chunk), f32),
            pltpu.VMEM((per_shard, window + 1, TILE, depth), f32),
            pltpu.VMEM((per_shard, window + 1, TILE, depth), f32),
            pltpu.VMEM((tiles, parts, share, depth), bf16),
            pltpu.VMEM((tiles, parts, share, depth), bf16),
        ]
        + [pltpu.VMEM((n_rail,) + shard, bf16)] * 6
        + [
            pltpu.VMEM((2, n_head, share, depth), bf16),
            pltpu.VMEM((2, n_head, share, depth), bf16),
            dma((2, 2, n_head)),
            dma((2, 2, n_rail, n_head)),
            dma((2, 2, n_head)),
            dma((2, 2, n_rail)),
            dma((2, 2, n_rail)),
            dma((2, 2, n_rail)),
            dma((2, 2, n_head)),
        ],
        compiler_params=pltpu.CompilerParams(
            collective_id=0, has_side_effects=True, vmem_limit_bytes=VMEM_LIMIT
        ),
        name="attention_all",
    )(
        tile_order,
        doc_tiles,
        queries.reshape(nch, chunk, depth),
        out_grad.reshape(nch, chunk, depth),
        key_proj.reshape(share, kv_heads * depth),
        value_proj.reshape(share, kv_heads * depth),
    )
    return (
        attended.reshape(row_count, group, depth),
        query_grad.reshape(row_count, group, depth),
        key_grad.reshape(share, kv_heads, depth),
        value_grad.reshape(share, kv_heads, depth),
    )


def solution(mesh):
    in_specs = (
        P("ctx", "head", None),
        P(("ctx", "head"), None, None),
        P(("ctx", "head"), None, None),
        P("ctx", "head", None),
        P(),
        P(),
    )
    out_specs = (
        P("ctx", "head", None),
        P("ctx", "head", None),
        P(("ctx", "head"), None, None),
        P(("ctx", "head"), None, None),
    )
    return jax.shard_map(
        functools.partial(body, mesh.shape["ctx"], mesh.shape["head"]),
        mesh=mesh,
        in_specs=in_specs,
        out_specs=out_specs,
        check_vma=False,
    )
```

time: 185 us -> 56.5 us (0.31)
  Pallas kernels: 0 us -> 49.1 us
  waiting for transfers between devices: 43.8 us -> 0 us
  other arithmetic: 43.5 us -> 0 us
  matrix products: 38.5 us -> 0 us
  starting transfers between devices: 33.8 us -> 0 us
  local copies, waits for them, and re-layouts: 21 us -> 6.51 us
    pallas_call x0 -> x1, Pallas kernels: none -> 49.1 us  [body(): pl.pallas_call(functools.partial(fused_kernel, n_ctx, n_head, tiles, grou...]
    dot_general x56 -> x0, matrix products: 38.5 us -> none  [the longest x16 13.9 us: block_scores(): jnp.einsum('tngd,knd->tngk', query_block, key_block, preferred_element_ty...]
    ppermute x46 -> x0, waiting for transfers between devices: 34.9 us -> none  [from_behind(): return lax.ppermute(value, axis, pairs)]
    ppermute x46 -> x0, starting transfers between devices: 18.8 us -> none  [from_behind(): return lax.ppermute(value, axis, pairs)]
    all_to_all x4 -> x0, starting transfers between devices: 15 us -> none  [the longest x1 5.16 us: body(): lax.all_to_all(key_proj, 'head', split_axis=1, concat_axis=0, tiled=True)]
    reduce_sum x25 -> x0, other arithmetic: 14.6 us -> none  [the longest x16 7.69 us: row_info(): jnp.sum((shard_tiles[:, None] >= doc_ends[None, :]).astype(jnp.int32), ax...]
    le x15 -> x0, other arithmetic: 9.68 us -> none  [block_mask(): key_pos[None, :] <= query_pos[:, None]]
    while x37 -> x0, local copies, waits for them, and re-layouts: 8.95 us -> none
  transfers between devices with their start and end apart: 50 -> 0, of which waited for: 27 -> 0; matrix products, arithmetic and copies ran while one was open for 43% -> 0% of each run, Pallas kernels for 0% -> 0%
where the time goes in v3:
time: 56.5 us; the launch traced here: 56.2 us
  Pallas kernels  49.1 us (87%)
  local copies, waits for them, and re-layouts  6.51 us (12%)
  between operations  0.66 us (1%)
    pallas_call x1, Pallas kernels, body(): pl.pallas_call(functools.partial(fused_kernel, n_ctx, n_head, tiles, grou...  49.1 us
    unnamed x10, local copies, waits for them, and re-layouts  4.33 us

profile of v3, /device:TPU:0, one launch (start us, length us, event | category | flops | bytes accessed | tf_op | source)
XLA Modules:
  0.0 56.2 jit_solution(5464026960359314507)
XLA Ops:
  0.6 0.9 %copy_bitcast_fusion = (bf16[64,512]{1,0:T(8,128)(2,1)S(1)}, bf16[64,512]{1,0:T(8,128)(2,1)S(1)}) fusion(bf16[8,8,4,128]{3,2,1,0:T(4,128)(2,1)} %bitcast.14, bf16[8,8,4,128]{3,2,1,0:T(4,128)(2,1)} %bitcast.15), kind=kLoop, calls=%fused_computation | loop fusion | bytes 262144 | tf_op jit(solution)/shard_map/reshape | solution.py:393
  1.5 0.0 copy-start.2
  1.5 0.0 copy-start.3
  1.5 0.6 %copy-done.2 = s32[16]{0:T(128)S(1)} copy-done((s32[16]{0:T(128)S(1)}, s32[16]{0:T(128)}, u32[]{:S(2)}) %copy-start.2) | copy-done | bytes 88
  2.2 0.0 copy-done.3
  2.2 0.0 copy-start
  2.2 1.0 %copy-done = bf16[256,8,128]{2,1,0:T(8,128)(2,1)S(1)} copy-done((bf16[256,8,128]{2,1,0:T(8,128)(2,1)S(1)}, bf16[256,8,128]{2,1,0:T(8,128)(2,1)}, u32[]{:S(2)}) %copy-start) | copy-done | bytes 524312
  3.2 0.0 copy-start.1
  3.2 1.0 %copy-done.1 = bf16[256,8,128]{2,1,0:T(8,128)(2,1)S(1)} copy-done((bf16[256,8,128]{2,1,0:T(8,128)(2,1)S(1)}, bf16[256,8,128]{2,1,0:T(8,128)(2,1)}, u32[]{:S(2)}) %copy-start.1) | copy-done | bytes 524312
  4.3 49.1 %attention_all.1 = (bf16[8,256,128]{2,1,0:T(8,128)(2,1)S(1)}, bf16[8,256,128]{2,1,0:T(8,128)(2,1)S(1)}, bf16[64,512]{1,0:T(8,128)(2,1)S(1)}, bf16[64,512]{1,0:T(8,128)(2,1)S(1)}) custom-call(s32[16]{0:T(128)S(1)} %copy-done.2, s32[4]{0:T(128)S(1)} %copy-done.3, bf16[8,256,128]{2,1,0:T(8,128)(2,1)S(1)} %bitcast.12, bf16[8,256,128]{2,1,0:T(8,128)(2,1)S(1)} %bitcast.13, ...), custom_call_target="tpu_custom_call" | custom-call | tf_op jit(solution)/shard_map/attention_all/pallas_call | solution.py:344
  53.3 0.6 %reshape.38 = bf16[64,4,128]{2,1,0:T(4,128)(2,1)} reshape(bf16[64,512]{1,0:T(8,128)(2,1)S(1)} %get-tuple-element.10) | data formatting | bytes 131072 | tf_op jit(solution)/shard_map/reshape | solution.py:398
  54.0 0.6 %reshape.39 = bf16[64,4,128]{2,1,0:T(4,128)(2,1)} reshape(bf16[64,512]{1,0:T(8,128)(2,1)S(1)} %get-tuple-element.11) | data formatting | bytes 131072 | tf_op jit(solution)/shard_map/reshape | solution.py:399
  54.6 0.8 %copy.16 = bf16[256,8,128]{2,1,0:T(8,128)(2,1)} copy(bf16[256,8,128]{2,1,0:T(8,128)(2,1)S(1)} %bitcast.11) | data formatting | bytes 1048576
  55.4 0.8 %copy.17 = bf16[256,8,128]{2,1,0:T(8,128)(2,1)} copy(bf16[256,8,128]{2,1,0:T(8,128)(2,1)S(1)} %bitcast.10) | data formatting | bytes 1048576
Async XLA Ops:
  1.5 0.7 %copy-start.2 = (s32[16]{0:T(128)S(1)}, s32[16]{0:T(128)}, u32[]{:S(2)}) copy-start(s32[16]{0:T(128)} %order_ref.1) | copy-start | bytes 196
  1.5 0.7 %copy-start.3 = (s32[4]{0:T(128)S(1)}, s32[4]{0:T(128)}, u32[]{:S(2)}) copy-start(s32[4]{0:T(128)} %docs_ref.1) | copy-start | bytes 52
  2.2 1.0 %copy-start = (bf16[256,8,128]{2,1,0:T(8,128)(2,1)S(1)}, bf16[256,8,128]{2,1,0:T(8,128)(2,1)}, u32[]{:S(2)}) copy-start(bf16[256,8,128]{2,1,0:T(8,128)(2,1)} %param.6) | copy-start | bytes 1572868
  3.2 1.0 %copy-start.1 = (bf16[256,8,128]{2,1,0:T(8,128)(2,1)S(1)}, bf16[256,8,128]{2,1,0:T(8,128)(2,1)}, u32[]{:S(2)}) copy-start(bf16[256,8,128]{2,1,0:T(8,128)(2,1)} %param.9) | copy-start | bytes 1572868

commit v4 on v3

--- a/solution.py
+++ b/solution.py
@@ -124,13 +124,15 @@
     for x in range(2):
         for d in range(1, n_head):
             head_copy(x, d).start()
-    for x in range(2):
+    def spread(x):
         for d in range(n_head):
             if d > 0:
                 head_copy(x, d).wait_recv()
             for dz in range(n_rail - 1, 0, -1):
                 rail_copy(x, dz, d).start()
             sib_copy(x, d).start()
+
+    spread(0)
 
     mine, count = [], []
     for t in range(per_shard):
@@ -164,6 +166,7 @@
                 turned_into[t, w] = block.T
 
     hand_on(0)
+    spread(1)
     arrive(0)
     fill(kw, kw_t, k_buf)
 

time: 56.5 us -> 54.1 us (0.958)
  Pallas kernels: 49.1 us -> 46.6 us
    pallas_call x1, Pallas kernels: 49.1 us -> 46.6 us  [body(): pl.pallas_call(functools.partial(fused_kernel, n_ctx, n_head, tiles, grou...]
where the time goes in v4:
time: 54.1 us; the launch traced here: 53.8 us
  Pallas kernels  46.6 us (86%)
  local copies, waits for them, and re-layouts  6.51 us (12%)
  between operations  0.66 us (1%)
    pallas_call x1, Pallas kernels, body(): pl.pallas_call(functools.partial(fused_kernel, n_ctx, n_head, tiles, grou...  46.6 us
    unnamed x10, local copies, waits for them, and re-layouts  4.33 us

profile of v4, /device:TPU:0, one launch (start us, length us, event | category | flops | bytes accessed | tf_op | source)
XLA Modules:
  0.0 53.8 jit_solution(2078962750166717649)
XLA Ops:
  0.6 0.9 %copy_bitcast_fusion = (bf16[64,512]{1,0:T(8,128)(2,1)S(1)}, bf16[64,512]{1,0:T(8,128)(2,1)S(1)}) fusion(bf16[8,8,4,128]{3,2,1,0:T(4,128)(2,1)} %bitcast.14, bf16[8,8,4,128]{3,2,1,0:T(4,128)(2,1)} %bitcast.15), kind=kLoop, calls=%fused_computation | loop fusion | bytes 262144 | tf_op jit(solution)/shard_map/reshape | solution.py:396
  1.5 0.0 copy-start.2
  1.5 0.0 copy-start.3
  1.5 0.6 %copy-done.2 = s32[16]{0:T(128)S(1)} copy-done((s32[16]{0:T(128)S(1)}, s32[16]{0:T(128)}, u32[]{:S(2)}) %copy-start.2) | copy-done | bytes 88
  2.2 0.0 copy-done.3
  2.2 0.0 copy-start
  2.2 1.0 %copy-done = bf16[256,8,128]{2,1,0:T(8,128)(2,1)S(1)} copy-done((bf16[256,8,128]{2,1,0:T(8,128)(2,1)S(1)}, bf16[256,8,128]{2,1,0:T(8,128)(2,1)}, u32[]{:S(2)}) %copy-start) | copy-done | bytes 524312
  3.2 0.0 copy-start.1
  3.2 1.0 %copy-done.1 = bf16[256,8,128]{2,1,0:T(8,128)(2,1)S(1)} copy-done((bf16[256,8,128]{2,1,0:T(8,128)(2,1)S(1)}, bf16[256,8,128]{2,1,0:T(8,128)(2,1)}, u32[]{:S(2)}) %copy-start.1) | copy-done | bytes 524312
  4.3 46.6 %attention_all.1 = (bf16[8,256,128]{2,1,0:T(8,128)(2,1)S(1)}, bf16[8,256,128]{2,1,0:T(8,128)(2,1)S(1)}, bf16[64,512]{1,0:T(8,128)(2,1)S(1)}, bf16[64,512]{1,0:T(8,128)(2,1)S(1)}) custom-call(s32[16]{0:T(128)S(1)} %copy-done.2, s32[4]{0:T(128)S(1)} %copy-done.3, bf16[8,256,128]{2,1,0:T(8,128)(2,1)S(1)} %bitcast.12, bf16[8,256,128]{2,1,0:T(8,128)(2,1)S(1)} %bitcast.13, ...), custom_call_target="tpu_custom_call" | custom-call | tf_op jit(solution)/shard_map/attention_all/pallas_call | solution.py:347
  50.9 0.6 %reshape.38 = bf16[64,4,128]{2,1,0:T(4,128)(2,1)} reshape(bf16[64,512]{1,0:T(8,128)(2,1)S(1)} %get-tuple-element.10) | data formatting | bytes 131072 | tf_op jit(solution)/shard_map/reshape | solution.py:401
  51.6 0.6 %reshape.39 = bf16[64,4,128]{2,1,0:T(4,128)(2,1)} reshape(bf16[64,512]{1,0:T(8,128)(2,1)S(1)} %get-tuple-element.11) | data formatting | bytes 131072 | tf_op jit(solution)/shard_map/reshape | solution.py:402
  52.2 0.8 %copy.16 = bf16[256,8,128]{2,1,0:T(8,128)(2,1)} copy(bf16[256,8,128]{2,1,0:T(8,128)(2,1)S(1)} %bitcast.11) | data formatting | bytes 1048576
  53.0 0.8 %copy.17 = bf16[256,8,128]{2,1,0:T(8,128)(2,1)} copy(bf16[256,8,128]{2,1,0:T(8,128)(2,1)S(1)} %bitcast.10) | data formatting | bytes 1048576
Async XLA Ops:
  1.5 0.7 %copy-start.2 = (s32[16]{0:T(128)S(1)}, s32[16]{0:T(128)}, u32[]{:S(2)}) copy-start(s32[16]{0:T(128)} %order_ref.1) | copy-start | bytes 196
  1.5 0.7 %copy-start.3 = (s32[4]{0:T(128)S(1)}, s32[4]{0:T(128)}, u32[]{:S(2)}) copy-start(s32[4]{0:T(128)} %docs_ref.1) | copy-start | bytes 52
  2.2 1.0 %copy-start = (bf16[256,8,128]{2,1,0:T(8,128)(2,1)S(1)}, bf16[256,8,128]{2,1,0:T(8,128)(2,1)}, u32[]{:S(2)}) copy-start(bf16[256,8,128]{2,1,0:T(8,128)(2,1)} %param.6) | copy-start | bytes 1572868
  3.2 1.0 %copy-start.1 = (bf16[256,8,128]{2,1,0:T(8,128)(2,1)S(1)}, bf16[256,8,128]{2,1,0:T(8,128)(2,1)}, u32[]{:S(2)}) copy-start(bf16[256,8,128]{2,1,0:T(8,128)(2,1)} %param.9) | copy-start | bytes 1572868
